TPU v7x, 32 devices: a whole 2x2x4 slice. The times are simulated.
32 devices in a mesh: grp: 4 (over z), shard: 8 (over y, x, core).
Axes of the slice: x: 2, y: 2, z: 4, core: 2. Of those that a mesh axis runs over, the one named last changes fastest.
Arguments:
- patches: bfloat16 [8192, 16], P(('grp', 'shard')), may hold values from -6 to 6
- noise: float32 [8192, 16], P(('grp', 'shard')), may hold values from -6 to 6
- timesteps: int32 [32], P(('grp', 'shard')), may hold values from 0 to 999
- labels: int32 [32], P(('grp', 'shard')), may hold values from 0 to 999
- assign: int32 [288], replicated, may hold values from 0 to 287, each once
- tile_master: float32 [288, 256, 256], P('shard'), may hold values from -0.1875 to 0.1875
- tile_bases: float32 [288, 2, 256, 256], P('shard'), may hold values from -1 to 1, as said below
- tile_moment: float32 [288, 256, 256], P('shard'), may hold values from -0.0007324219 to 0.0007324219
- tile_second: float32 [288, 256, 256], P('shard'), may hold values from 3e-10 to 1e-08
- row_master: float32 [4379, 1024], P(None, 'shard'), may hold values from -1.5 to 1.5
- row_moment: float32 [4379, 1024], P(None, 'shard'), may hold values from -0.0007324219 to 0.0007324219
- row_second: float32 [4379, 1024], P(None, 'shard'), may hold values from 3e-10 to 1e-08
Outputs:
- loss: float32 [], replicated
- grad_norm: float32 [], replicated
- act_rms: float32 [3], replicated
- new_tile_moment: float32 [288, 256, 256], P('shard')
- new_tile_second: float32 [288, 256, 256], P('shard')
- tile_update: float32 [288, 256, 256], P('shard')
- new_row_moment: float32 [4379, 1024], P(None, 'shard')
- new_row_second: float32 [4379, 1024], P(None, 'shard')
- row_update: float32 [4379, 1024], P(None, 'shard')
Inputs may be any that keep to these rules, and one draw needn't show every extreme that they name: assign is a permutation: each block stands in exactly one slot; slot s belongs to the owner s // 36. tile_bases[s, 0] and tile_bases[s, 1] are orthogonal matrices.
All inputs are finite; a program needn't handle non-finite values.
Results may differ from a plain program's by a relative error of at most 0.018.
Values may be sent and summed in bfloat16 or wider, within the bound.
A program may use at most 448 MiB of HBM per device.

v0:
```python
import math

import jax
import jax.numpy as jnp
from jax import lax
from jax.sharding import PartitionSpec as P

D = 1024
HEADS = 16
HD = 64
FF = 4096
NCLASS = 1000
FREQ = 256
PATCH_SIDE = 2
LAT = 32
BLK = 256
PATCH_DIM = 16
SEQ = 256


highest = lax.Precision.HIGHEST
ln_eps = 1e-06
beta_one = 0.5
beta_two = 0.5
adam_eps = 1e-08
rate_step = 0.01
decay_rate = 0.1
clip_at = 0.25


def untile(block, row_count, col_count, tile_edge):
    shaped = block.reshape(row_count // tile_edge, col_count // tile_edge, tile_edge, tile_edge)
    return shaped.transpose(0, 2, 1, 3).reshape(row_count, col_count)


def matrix_shapes(model_width, hidden_width):
    return [
        (model_width, 6 * model_width),
        (model_width, 3 * model_width),
        (model_width, model_width),
        (model_width, hidden_width),
        (hidden_width, model_width),
    ]


def split_matrices(tiles, model_width, hidden_width, tile_edge):
    result = []
    offset = 0
    for row_count, col_count in matrix_shapes(model_width, hidden_width):
        tile_count = row_count // tile_edge * (col_count // tile_edge)
        result.append(untile(tiles[offset : offset + tile_count], row_count, col_count, tile_edge))
        offset += tile_count
    return result


def split_rows(row_block, model_width, hidden_width, class_count, freq_width, patch_width):
    sizes_list = [
        class_count,
        freq_width,
        model_width,
        2 * model_width,
        patch_width,
        patch_width,
        1,
        1,
        1,
        1,
        1,
        1,
        1,
        6,
        hidden_width // model_width,
        2,
    ]
    pieces = []
    offset = 0
    for row_count in sizes_list:
        pieces.append(row_block[offset : offset + row_count])
        offset += row_count
    final_rows = pieces[3]
    w_final = jnp.concatenate([final_rows[:model_width], final_rows[model_width:]], axis=1)
    vectors = [piece.reshape(-1) for piece in pieces[6:]]
    return [pieces[0], pieces[1], pieces[2], w_final, pieces[4], pieces[5]] + vectors


def positions(grid_side, model_width):
    index = jnp.arange(grid_side * grid_side)
    row_pos = (index // grid_side).astype(jnp.float32)
    col_pos = (index % grid_side).astype(jnp.float32)
    quarter = model_width // 4
    omega = 1.0 / 10000.0 ** (jnp.arange(quarter, dtype=jnp.float32) / quarter)
    row_arg = row_pos[:, None] * omega[None, :]
    col_arg = col_pos[:, None] * omega[None, :]
    return jnp.concatenate(
        [jnp.sin(row_arg), jnp.cos(row_arg), jnp.sin(col_arg), jnp.cos(col_arg)], axis=1
    )


def time_freq(step_values, freq_width):
    half_width = freq_width // 2
    freqs = jnp.exp(-math.log(10000.0) * jnp.arange(half_width, dtype=jnp.float32) / half_width)
    angle_arg = step_values.astype(jnp.float32)[:, None] * freqs[None, :]
    return jnp.concatenate([jnp.cos(angle_arg), jnp.sin(angle_arg)], axis=1)


def layer_norm(hidden_in):
    centred = hidden_in - jnp.mean(hidden_in, axis=-1, keepdims=True)
    spread = jnp.mean(centred * centred, axis=-1, keepdims=True)
    return centred * lax.rsqrt(spread + ln_eps)


def modulate(hidden_in, scale_row, shift_row):
    return layer_norm(hidden_in) * (1.0 + scale_row[:, None, :]) + shift_row[:, None, :]


def gelu_tanh(values_in):
    return jax.nn.gelu(values_in, approximate=True)


def dense(left_in, weight):
    return jnp.dot(left_in, weight, preferred_element_type=jnp.float32)


def inner_grad(left_in, right_in):
    return lax.dot_general(
        left_in, right_in, (((0,), (0,)), ((), ())), preferred_element_type=jnp.float32
    )


def back_prod(grad_low, weight):
    return lax.dot_general(
        grad_low, weight, (((1,), (1,)), ((), ())), preferred_element_type=jnp.float32
    )


def tiled_grad(left_in, right_in, tile_edge):
    token_total = left_in.shape[0]
    left_view = left_in.reshape(token_total, left_in.shape[1] // tile_edge, tile_edge)
    right_view = right_in.reshape(token_total, right_in.shape[1] // tile_edge, tile_edge)
    tiles = jnp.einsum("nab,ncd->acbd", left_view, right_view, preferred_element_type=jnp.float32)
    return tiles.reshape(-1, tile_edge, tile_edge)


def shards(
    patches,
    noise,
    timesteps,
    labels,
    assign,
    tile_master,
    tile_bases,
    tile_moment,
    tile_second,
    row_master,
    row_moment,
    row_second,
):
    gathered_tiles, gathered_rows = (
        lax.all_gather(tile_master.astype(jnp.bfloat16), "shard", axis=0, tiled=True),
        lax.all_gather(row_master.astype(jnp.bfloat16), "shard", axis=1, tiled=True),
    )
    tile_total = gathered_tiles.shape[0]
    inverse = (
        jnp.zeros((tile_total,), jnp.int32).at[assign].set(jnp.arange(tile_total, dtype=jnp.int32))
    )
    w_ada, w_qkv, w_out, w_up, w_down = split_matrices(gathered_tiles[inverse], D, FF, BLK)
    (
        label_table,
        w_time1,
        w_time2,
        w_final,
        w_patch,
        w_head,
        b_patch,
        b_time1,
        b_time2,
        b_query,
        b_value,
        b_out,
        b_down,
        b_ada,
        b_up,
        b_final,
    ) = split_rows(gathered_rows, D, FF, NCLASS, FREQ, PATCH_DIM)
    image_count = timesteps.shape[0]
    token_count = patches.shape[0]
    token_total = token_count * lax.axis_size("grp") * lax.axis_size("shard")
    loss_scale = 1.0 / (token_total * PATCH_DIM)
    att_scale = HD ** (-0.5)
    head_shape = (image_count, SEQ, HEADS, HD)
    low_type = jnp.bfloat16
    embed = dense(patches, w_patch) + b_patch
    stream = embed.reshape(image_count, SEQ, D) + positions(LAT // PATCH_SIDE, D)[None]
    freq_low = time_freq(timesteps, FREQ).astype(low_type)
    time_pre = dense(freq_low, w_time1) + b_time1
    time_low = jax.nn.silu(time_pre).astype(low_type)
    time_embed = dense(time_low, w_time2) + b_time2
    one_hot = labels[:, None] == jnp.arange(NCLASS, dtype=jnp.int32)[None, :]
    condition = time_embed + dense(one_hot.astype(low_type), label_table)
    cond_low = jax.nn.silu(condition).astype(low_type)
    modulation = dense(cond_low, w_ada) + b_ada
    final_mod = dense(cond_low, w_final) + b_final
    shift_att, scale_att, gate_att, shift_mlp, scale_mlp, gate_mlp = jnp.split(
        modulation, 6, axis=1
    )
    shift_fin, scale_fin = jnp.split(final_mod, 2, axis=1)
    normed_att, back_att = jax.vjp(modulate, stream, scale_att, shift_att)
    att_low = normed_att.astype(low_type).reshape(token_count, D)
    qkv_all = dense(att_low, w_qkv)
    queries = (qkv_all[:, :D] + b_query).astype(low_type).reshape(head_shape)
    keys_all = qkv_all[:, D : 2 * D].astype(low_type).reshape(head_shape)
    values_all = (qkv_all[:, 2 * D :] + b_value).astype(low_type).reshape(head_shape)
    scores = (
        jnp.einsum("ilhd,imhd->ihlm", queries, keys_all, preferred_element_type=jnp.float32)
        * att_scale
    )
    log_total = jax.nn.logsumexp(scores, axis=-1)
    probs_low = jnp.exp(scores - log_total[..., None]).astype(low_type)
    attended = jnp.einsum(
        "ihlm,imhd->ilhd", probs_low, values_all, preferred_element_type=jnp.float32
    )
    attended = attended.reshape(token_count, D).astype(low_type)
    out_att = (dense(attended, w_out) + b_out).reshape(image_count, SEQ, D)
    branch_att = gate_att[:, None, :] * out_att
    stream_mid = stream + branch_att
    normed_mlp, back_mlp = jax.vjp(modulate, stream_mid, scale_mlp, shift_mlp)
    mlp_low = normed_mlp.astype(low_type).reshape(token_count, D)
    up_pre = dense(mlp_low, w_up) + b_up
    hidden_act, back_gelu = jax.vjp(gelu_tanh, up_pre)
    hidden_low = hidden_act.astype(low_type)
    out_mlp = (dense(hidden_low, w_down) + b_down).reshape(image_count, SEQ, D)
    branch_mlp = gate_mlp[:, None, :] * out_mlp
    stream_end = stream_mid + branch_mlp
    normed_end, back_end = jax.vjp(modulate, stream_end, scale_fin, shift_fin)
    end_low = normed_end.astype(low_type).reshape(token_count, D)
    predicted = back_prod(end_low, w_head)
    mismatch = predicted - noise
    statistics = jnp.stack(
        [
            jnp.sum(mismatch * mismatch),
            jnp.sum(stream_end * stream_end),
            jnp.sum(branch_att * branch_att),
            jnp.sum(branch_mlp * branch_mlp),
        ]
    )
    pred_low = (2.0 * loss_scale * mismatch).astype(low_type)
    grad_head = inner_grad(pred_low, end_low)
    end_grad = dense(pred_low, w_head).reshape(image_count, SEQ, D)
    end_stream_grad, scale_fin_grad, shift_fin_grad = back_end(end_grad)
    gate_mlp_grad = jnp.sum(end_stream_grad * out_mlp, axis=1)
    down_grad = (end_stream_grad * gate_mlp[:, None, :]).reshape(token_count, D)
    down_low = down_grad.astype(low_type)
    tiles_down = tiled_grad(hidden_low, down_low, BLK)
    up_grad = back_gelu(back_prod(down_low, w_down))[0]
    up_low = up_grad.astype(low_type)
    tiles_up = tiled_grad(mlp_low, up_low, BLK)
    mlp_grad = back_prod(up_low, w_up).reshape(image_count, SEQ, D)
    mid_part, scale_mlp_grad, shift_mlp_grad = back_mlp(mlp_grad)
    mid_grad = end_stream_grad + mid_part
    gate_att_grad = jnp.sum(mid_grad * out_att, axis=1)
    proj_grad = (mid_grad * gate_att[:, None, :]).reshape(token_count, D)
    proj_low = proj_grad.astype(low_type)
    tiles_out = tiled_grad(attended, proj_low, BLK)
    attended_grad = back_prod(proj_low, w_out).astype(low_type).reshape(head_shape)
    scores_again = (
        jnp.einsum("ilhd,imhd->ihlm", queries, keys_all, preferred_element_type=jnp.float32)
        * att_scale
    )
    probs = jnp.exp(scores_again - log_total[..., None])
    prob_grad = jnp.einsum(
        "ilhd,imhd->ihlm", attended_grad, values_all, preferred_element_type=jnp.float32
    )
    value_grad = jnp.einsum(
        "ihlm,ilhd->imhd", probs_low, attended_grad, preferred_element_type=jnp.float32
    )
    score_grad = probs * (prob_grad - jnp.sum(prob_grad * probs, axis=-1, keepdims=True))
    score_low = score_grad.astype(low_type)
    query_grad = (
        jnp.einsum("ihlm,imhd->ilhd", score_low, keys_all, preferred_element_type=jnp.float32)
        * att_scale
    )
    key_grad = (
        jnp.einsum("ihlm,ilhd->imhd", score_low, queries, preferred_element_type=jnp.float32)
        * att_scale
    )
    qkv_grad = jnp.concatenate(
        [
            query_grad.reshape(token_count, D),
            key_grad.reshape(token_count, D),
            value_grad.reshape(token_count, D),
        ],
        axis=1,
    )
    qkv_low = qkv_grad.astype(low_type)
    tiles_qkv = tiled_grad(att_low, qkv_low, BLK)
    att_in_grad = back_prod(qkv_low, w_qkv).reshape(image_count, SEQ, D)
    stream_part, scale_att_grad, shift_att_grad = back_att(att_in_grad)
    stream_grad = (mid_grad + stream_part).reshape(token_count, D)
    grad_patch = inner_grad(patches, stream_grad.astype(low_type))
    mod_grad = jnp.concatenate(
        [
            shift_att_grad,
            scale_att_grad,
            gate_att_grad,
            shift_mlp_grad,
            scale_mlp_grad,
            gate_mlp_grad,
        ],
        axis=1,
    )
    mod_low = mod_grad.astype(low_type)
    tiles_ada = tiled_grad(cond_low, mod_low, BLK)
    fin_grad = jnp.concatenate([shift_fin_grad, scale_fin_grad], axis=1)
    fin_low = fin_grad.astype(low_type)
    grad_final = inner_grad(cond_low, fin_low)
    cond_act_grad = back_prod(mod_low, w_ada) + back_prod(fin_low, w_final)
    cond_grad = jax.vjp(jax.nn.silu, condition)[1](cond_act_grad)[0]
    cond_grad_low = cond_grad.astype(low_type)
    grad_time2 = inner_grad(time_low, cond_grad_low)
    time_pre_grad = jax.vjp(jax.nn.silu, time_pre)[1](back_prod(cond_grad_low, w_time2))[0]
    grad_time1 = inner_grad(freq_low, time_pre_grad.astype(low_type))
    rest_rows = jnp.concatenate(
        [
            grad_time1,
            grad_time2,
            grad_final[:, :D],
            grad_final[:, D:],
            grad_patch,
            grad_head,
            jnp.sum(stream_grad, axis=0)[None],
            jnp.sum(time_pre_grad, axis=0)[None],
            jnp.sum(cond_grad, axis=0)[None],
            jnp.sum(qkv_grad[:, :D], axis=0)[None],
            jnp.sum(qkv_grad[:, 2 * D :], axis=0)[None],
            jnp.sum(proj_grad, axis=0)[None],
            jnp.sum(down_grad, axis=0)[None],
            jnp.sum(mod_grad, axis=0).reshape(6, D),
            jnp.sum(up_grad, axis=0).reshape(FF // D, D),
            jnp.sum(fin_grad, axis=0).reshape(2, D),
        ],
        axis=0,
    )
    grad_slots = jnp.concatenate([tiles_ada, tiles_qkv, tiles_out, tiles_up, tiles_down], axis=0)[
        assign
    ]
    label_grad = jnp.dot(one_hot.astype(jnp.float32).T, cond_grad, precision=highest)
    dense_rows = jnp.concatenate([label_grad, rest_rows], axis=0)
    own_tiles, own_rows = (
        lax.psum_scatter(
            grad_slots.astype(jnp.bfloat16), "shard", scatter_dimension=0, tiled=True
        ).astype(jnp.float32),
        lax.psum_scatter(
            dense_rows.astype(jnp.bfloat16), "shard", scatter_dimension=1, tiled=True
        ).astype(jnp.float32),
    )
    whole_stats = lax.psum(statistics, ("grp", "shard"))
    own_tiles, own_rows = (
        lax.psum(own_tiles.astype(jnp.bfloat16), "grp").astype(jnp.float32),
        lax.psum(own_rows.astype(jnp.bfloat16), "grp").astype(jnp.float32),
    )
    square_part = jnp.sum(own_tiles * own_tiles) + jnp.sum(own_rows * own_rows)
    square_sum = lax.psum(square_part, "shard")
    grad_norm = jnp.sqrt(square_sum)
    factor = clip_at / jnp.maximum(grad_norm, clip_at)
    tile_grad = factor * own_tiles
    left_basis = tile_bases[:, 0]
    right_basis = tile_bases[:, 1]
    rotated = jnp.einsum(
        "sji,sjk->sik",
        left_basis,
        jnp.einsum("sij,sjk->sik", tile_grad, right_basis, precision=highest),
        precision=highest,
    )
    new_tile_moment = beta_one * tile_moment + (1.0 - beta_one) * rotated
    new_tile_second = beta_two * tile_second + (1.0 - beta_two) * rotated * rotated
    direction = new_tile_moment / (jnp.sqrt(new_tile_second) + adam_eps)
    restored = jnp.einsum(
        "sij,skj->sik",
        jnp.einsum("sij,sjk->sik", left_basis, direction, precision=highest),
        right_basis,
        precision=highest,
    )
    tile_update = -rate_step * restored
    row_grad = factor * own_rows
    new_row_moment = beta_one * row_moment + (1.0 - beta_one) * row_grad
    new_row_second = beta_two * row_second + (1.0 - beta_two) * row_grad * row_grad
    row_update = -rate_step * (
        new_row_moment / (jnp.sqrt(new_row_second) + adam_eps) + decay_rate * row_master
    )
    loss = whole_stats[0] / (token_total * PATCH_DIM)
    act_rms = jnp.sqrt(whole_stats[1:] / (token_total * D))
    return (
        loss,
        grad_norm,
        act_rms,
        new_tile_moment,
        new_tile_second,
        tile_update,
        new_row_moment,
        new_row_second,
        row_update,
    )


def solution(mesh):
    placed = (
        P(("grp", "shard"), None),
        P(("grp", "shard"), None),
        P(("grp", "shard")),
        P(("grp", "shard")),
        P(),
        P("shard", None, None),
        P("shard", None, None, None),
        P("shard", None, None),
        P("shard", None, None),
        P(None, "shard"),
        P(None, "shard"),
        P(None, "shard"),
    )
    return jax.shard_map(
        shards,
        mesh=mesh,
        in_specs=placed,
        out_specs=(
            P(),
            P(),
            P(),
            P("shard", None, None),
            P("shard", None, None),
            P("shard", None, None),
            P(None, "shard"),
            P(None, "shard"),
            P(None, "shard"),
        ),
        check_vma=False,
    )
```

profile of v0, /device:TPU:0, one launch (start us, length us, event | category | flops | bytes accessed | tf_op | source)
XLA Modules:
  0.0 1275.5 jit_solution(3327034802856895632)
XLA Ops:
  7.2 2.7 convert_element_type.197
  10.1 6.5 convert_element_type.207
  19.2 2.9 scatter_custom_fusion
  24.1 47.7 %all-gather.3.cloned.1.call-done = bf16[4379,1024]{1,0:T(8,128)(2,1)} async-done(((bf16[4379,128]{1,0:T(8,128)(2,1)}), bf16[4379,1024]{1,0:T(8,128)(2,1)}) %all-gather.3.cloned.1.call-update) | async-done | bytes 8968208 | tf_op jit(solution)/shard_map/all_gather | solution.py:160
  83.6 3.6 fusion.108
  89.4 164.5 %all-gather.5.cloned.1.call-done = bf16[288,256,256]{2,1,0:T(8,128)(2,1)} async-done(((bf16[36,256,256]{2,1,0:T(8,128)(2,1)}), bf16[288,256,256]{2,1,0:T(8,128)(2,1)}) %all-gather.5.cloned.1.call-update) | async-done | bytes 37748752 | tf_op jit(solution)/shard_map/all_gather | solution.py:159
  253.9 27.0 %gather_fusion = bf16[288,256,256]{2,1,0:T(8,128)(2,1)} fusion(bf16[288,256,256]{2,1,0:T(8,128)(2,1)} %all-gather.5.cloned.1.call-done, s32[1024]{0:T(1024)S(1)} %pad_clamp_fusion.1), kind=kCustom, calls=%fused_computation | custom fusion | bytes 75498624 | tf_op jit(solution)/shard_map/gather | solution.py:166
  280.9 6.2 slice.143
  287.1 12.6 fusion.107
  299.7 2.6 slice-done.3
  302.4 31.7 %copy.76 = bf16[4,24,256,256]{3,1,2,0:T(8,128)(2,1)S(1)} copy(bf16[4,24,256,256]{3,2,1,0:T(8,128)(2,1)S(1)} %bitcast.234) | data formatting | bytes 25165824 | tf_op jit(solution)/shard_map/reshape | solution.py:32
  334.1 10.0 copy.130
  345.8 2.8 copy-done.2
  348.7 10.7 copy.77
  359.4 4.8 copy.131
  370.3 2.1 multiply_reduce_fusion.1
  375.1 2.1 copy.78
  382.4 12.0 copy.83
  394.5 12.4 copy.133
  406.9 14.7 %copy.84 = bf16[16,4,256,256]{2,0,3,1:T(8,128)(2,1)} copy(bf16[16,4,256,256]{3,2,1,0:T(8,128)(2,1)} %bitcast.243) | data formatting | bytes 16777216 | tf_op jit(solution)/shard_map/reshape | solution.py:32
  421.6 12.4 copy.135
  434.3 9.1 multiply_convert_fusion.3
  443.4 2.5 fusion.105
  448.1 2.5 multiply_reduce_fusion.3
  452.0 4.8 fusion.93
  456.9 2.7 multiply_reduce_fusion.5
  463.9 3.5 multiply_reduce_fusion
  472.0 2.1 multiply_reduce_fusion.2
  477.2 3.5 fusion.116
  482.4 2.2 fusion.35
  485.2 2.5 fusion.109
  490.0 41.3 %concatenate.93 = bf16[4379,1024]{1,0:T(8,128)(2,1)} concatenate(bf16[1000,1024]{1,0:T(8,128)(2,1)} %multiply_convert_fusion.4, bf16[256,1024]{1,0:T(8,128)(2,1)S(1)} %multiply_convert_fusion.5, bf16[1024,1024]{1,0:T(8,128)(2,1)S(1)} %multiply_convert_fusion.1, bf16[1024,1024]{1,0:T(8,128)(2,1)} %get-tuple-element.98, bf16[1024,1024]{1,0:T(8,128)(2,1)} %get-tuple-element.97, ...), dimensions={0} | concatenate | bytes 17936384 | tf_op jit(solution)/shard_map/concatenate | solution.py:347
  531.3 12.3 copy.123
  545.7 2.5 copy.121
  549.5 3.1 convolution_bitcast_fusion.3
  552.7 3.1 copy.93
  555.8 6.5 convolution_bitcast_fusion.2
  562.3 8.9 copy.90
  571.2 7.4 convolution_bitcast_fusion.1
  578.7 11.7 copy.96
  590.3 7.4 convolution_bitcast_fusion
  597.7 11.8 copy.99
  609.5 9.0 broadcast_multiply_fusion
  618.6 11.0 constant_dynamic-update-slice_fusion.4
  629.6 3.3 constant_dynamic-update-slice_fusion.3
  634.4 7.7 constant_dynamic-update-slice_fusion.1
  642.0 7.7 constant_dynamic-update-slice_fusion
  649.7 27.0 %gather_fusion.1 = bf16[288,256,256]{2,1,0:T(8,128)(2,1)} fusion(bf16[288,256,256]{2,1,0:T(8,128)(2,1)} %constant_dynamic-update-slice_fusion, s32[1024]{0:T(1024)S(1)} %pad_clamp_fusion), kind=kCustom, calls=%fused_computation.1 | custom fusion | bytes 75498624 | tf_op jit(solution)/shard_map/gather | solution.py:343
  676.9 2.4 copy.124
  679.2 223.0 %reduce-scatter.5.cloned.1.call-done = bf16[36,256,256]{2,1,0:T(8,128)(2,1)} async-done(((bf16[288,256,256]{2,1,0:T(8,128)(2,1)}), bf16[36,256,256]{2,1,0:T(8,128)(2,1)}) %reduce-scatter.5.cloned.1.call-update) | async-done | bytes 4718608 | tf_op jit(solution)/shard_map/reduce_scatter | solution.py:349
  902.2 9.7 copy.100
  911.9 2.6 pad_maximum_fusion.5
  914.6 9.6 copy.104
  924.1 43.5 %psum.28 = f32[4]{0:T(128)S(1)} all-reduce(f32[4]{0:T(128)S(1)} %pad_maximum_fusion.5), channel_id=1, replica_groups=mesh['grp'=4,'shard'=8] {'grp','shard'}, use_global_device_ids=true, to_apply=%region_13.14 | all-reduce | flops 4 | bytes 32 | tf_op jit(solution)/shard_map/psum | solution.py:356
  968.3 146.8 %all-reduce.3.cloned.1.call-done = (bf16[36,256,256]{2,1,0:T(8,128)(2,1)}, bf16[4379,128]{1,0:T(8,128)(2,1)}) async-done(((bf16[36,256,256]{2,1,0:T(8,128)(2,1)}, bf16[4379,128]{1,0:T(8,128)(2,1)}), (bf16[36,256,256]{2,1,0:T(8,128)(2,1)}, bf16[4379,128]{1,0:T(8,128)(2,1)})) %all-reduce.3.cloned.1.call-update) | async-done | bytes 5839632 | tf_op jit(solution)/shard_map/psum | solution.py:358
  1115.0 5.5 fusion
  1123.0 14.5 %psum.31 = f32[]{:T(128)} all-reduce(f32[]{:T(128)S(6)} %add.375), channel_id=1, replica_groups=mesh['grp'=4,'shard'=8] {'shard'}, use_global_device_ids=true, to_apply=%region_41.42 | all-reduce | flops 1 | bytes 8 | tf_op jit(solution)/shard_map/psum | solution.py:362
  1138.3 27.2 %fusion.1 = f32[36,256,256]{1,2,0:T(8,128)} fusion(bf16[36,256,256]{2,1,0:T(8,128)(2,1)} %get-tuple-element.53, f32[36,2,256,256]{3,2,1,0:T(8,128)} %param.18, f32[]{:T(128)S(6)} %div.142), kind=kOutput, calls=%fused_computation.9 | convolution fusion | flops 7252475904 | bytes 23592964 | tf_op jit(solution)/shard_map/sij,sjk->sik/dot_general | solution.py:371
  1165.5 28.8 %fusion.2 = (f32[36,256,256]{1,2,0:T(8,128)}, f32[36,256,256]{1,2,0:T(8,128)}) fusion(f32[36,256,256]{1,2,0:T(8,128)} %copy.104, f32[36,256,256]{1,2,0:T(8,128)} %copy.100, f32[36,256,256]{1,2,0:T(8,128)} %fusion.1, f32[36,2,256,256]{3,2,1,0:T(8,128)} %param.18), kind=kOutput, calls=%fused_computation.10 | convolution fusion | flops 7261913088 | bytes 56623104 | tf_op jit(solution)/shard_map/sji,sjk->sik/dot_general | solution.py:368
  1194.2 9.6 copy.106
  1203.8 20.5 %fusion.3 = f32[36,256,256]{1,2,0:T(8,128)} fusion(f32[36,256,256]{1,2,0:T(8,128)} %get-tuple-element.87, f32[36,256,256]{1,2,0:T(8,128)} %get-tuple-element.86, f32[36,2,256,256]{3,2,1,0:T(8,128)} %param.18), kind=kOutput, calls=%fused_computation.11 | convolution fusion | flops 7252475904 | bytes 37748736 | tf_op jit(solution)/shard_map/sij,sjk->sik/dot_general | solution.py:379
  1224.3 9.6 copy.107
  1233.9 28.2 %broadcast_multiply_fusion.1 = f32[36,256,256]{2,1,0:T(8,128)} fusion(f32[36,256,256]{1,2,0:T(8,128)} %fusion.3, f32[36,2,256,256]{3,2,1,0:T(8,128)} %param.18), kind=kOutput, calls=%fused_computation.31 | convolution fusion | flops 7250116608 | bytes 28311552 | tf_op jit(solution)/shard_map/sij,skj->sik/dot_general | solution.py:377
  1262.1 4.2 add_multiply_fusion
  (283 shorter events, 59.7 us)
Async XLA Ops:
  7.2 74.2 %copy-start = (bf16[256,16]{0,1:T(8,128)(2,1)S(1)}, bf16[256,16]{0,1:T(8,128)(2,1)}, u32[]{:S(2)}) copy-start(bf16[256,16]{0,1:T(8,128)(2,1)} %param.12) | copy-start | bytes 24580
  7.2 64.6 %all-gather.3.cloned.1.call-start = ((), (), s32[]{:S(2)}) async-start(), calls=%async_computation.2 | async-start | bytes 10100736 | tf_op jit(solution)/shard_map/all_gather | solution.py:160
  10.0 243.9 %all-gather.5.cloned.1.call-start = ((), (), s32[]{:S(2)}) async-start(), calls=%async_computation.3 | async-start | bytes 42467328 | tf_op jit(solution)/shard_map/all_gather | solution.py:159
  16.6 2.6 copy-start.55
  16.6 660.2 %reduce-scatter.7.cloned.1.call-start = ((), (), s32[]{:S(2)}) async-start(), calls=%async_computation.5 | async-start | bytes 10321920
  19.2 3.0 copy-start.52
  72.8 6.5 copy-start.41
  76.7 2.6 copy-start.37
  82.8 4.4 copy-start.50
  87.2 1.4 copy-start.27
  87.2 2.2 copy-start.29
  287.1 15.3 %slice-start.3 = ((bf16[288,256,256]{2,1,0:T(8,128)(2,1)}), bf16[96,256,256]{2,1,0:T(8,128)(2,1)S(1)}, s32[]{:S(2)}) async-start(bf16[288,256,256]{2,1,0:T(8,128)(2,1)} %gather_fusion), calls=%async_computation.10 | async-start | bytes 25165824 | tf_op jit(solution)/shard_map/slice | solution.py:51
  344.1 4.5 copy-start.2
  364.2 2.6 copy-start.9
  364.5 2.5 copy-start.34
  370.3 7.0 slice-start.4
  372.4 2.0 copy-start.3
  377.2 2.2 copy-start.4
  377.2 2.3 copy-start.10
  379.4 2.8 copy-start.7
  380.4 14.1 %copy-start.12 = (bf16[16,64,256]{2,1,0:T(8,128)(2,1)}, bf16[16,64,256]{2,1,0:T(8,128)(2,1)S(1)}, u32[]{:S(2)}) copy-start(bf16[16,64,256]{2,1,0:T(8,128)(2,1)S(1)} %convolution_convert_fusion.1) | copy-start | bytes 1572868
  434.0 9.4 slice-start.9
  434.2 9.1 copy-start.32
  434.3 9.1 slice-start.10
  443.4 2.6 copy-start.31
  443.4 3.1 copy-start.48
  446.5 5.5 copy-start.14
  448.1 3.9 copy-start.56
  451.1 5.7 slice-start.7
  452.0 4.8 copy-start.24
  452.0 4.9 slice-start.8
  456.8 2.7 copy-start.22
  459.5 1.6 copy-start.8
  460.0 4.0 copy-start.11
  463.9 3.6 copy-start.5
  467.5 1.7 copy-start.16
  468.6 3.2 slice-start.11
  469.2 1.8 copy-start.35
  469.2 2.7 slice-start.12
  470.0 4.0 copy-start.36
  472.0 2.1 copy-start.51
  472.0 4.8 slice-start
  472.0 4.8 slice-start.1
  474.1 1.6 copy-start.19
  474.1 3.0 slice-start.2
  477.2 3.6 copy-start.28
  477.2 3.6 copy-start.30
  480.7 1.4 copy-start.15
  480.7 3.9 copy-start.49
  480.7 4.0 copy-start.47
  485.2 2.8 copy-start.46
  485.2 3.1 copy-start.54
  485.2 3.2 copy-start.45
  543.6 2.1 copy-start.23
  543.6 5.9 copy-start.13
  543.6 358.6 %reduce-scatter.5.cloned.1.call-start = ((), (), s32[]{:S(2)}) async-start(), calls=%async_computation.4 | async-start | bytes 42467328 | tf_op jit(solution)/shard_map/reduce_scatter | solution.py:349
  609.5 20.0 %slice-start.5 = ((s8[6291456]{0:T(1024)(128)(4,1)}), s8[2097152]{0:T(1024)(128)(4,1)S(1)}, s32[]{:S(2)}) async-start(s8[6291456]{0:T(1024)(128)(4,1)} %bitcast.245), calls=%async_computation.12 | async-start | bytes 4194304
  618.6 11.0 slice-start.6
  676.8 438.2 %all-reduce.3.cloned.1.call-start = ((), (), s32[]{:S(2)}) async-start(), calls=%async_computation.6 | async-start | bytes 11681792 | tf_op jit(solution)/shard_map/psum | solution.py:358
  1115.0 5.5 copy-start.18
  1233.9 28.2 %copy-start.6 = (f32[4379,128]{1,0:T(8,128)S(1)}, f32[4379,128]{1,0:T(8,128)}, u32[]{:S(2)}) copy-start(f32[4379,128]{1,0:T(8,128)} %param.21) | copy-start | bytes 6726148
  1233.9 28.2 %copy-start.20 = (f32[4379,128]{1,0:T(8,128)S(1)}, f32[4379,128]{1,0:T(8,128)}, u32[]{:S(2)}) copy-start(f32[4379,128]{1,0:T(8,128)} %param.23) | copy-start | bytes 6726148
  1233.9 28.2 %copy-start.21 = (f32[4379,128]{1,0:T(8,128)S(1)}, f32[4379,128]{1,0:T(8,128)}, u32[]{:S(2)}) copy-start(f32[4379,128]{1,0:T(8,128)} %param.22) | copy-start | bytes 6726148
  1233.9 32.3 %copy-start.1 = (bf16[256,16]{0,1:T(8,128)(2,1)S(1)}, bf16[256,16]{0,1:T(8,128)(2,1)}, u32[]{:S(2)}) copy-start(bf16[256,16]{0,1:T(8,128)(2,1)} %param.12) | copy-start | bytes 24580
  (11 other events, 10.1 us)
Sparse Core Ops, SparseCore 0:
  10.5 61.2 all-gather.2
  74.3 179.5 all-gather.4
  543.7 75.0 reduce-scatter.6
  676.9 225.2 reduce-scatter.4
  905.1 209.8 all-reduce.2
where the time goes:
time: 1290 us; the launch traced here: 1280 us
  waiting for transfers between devices  582 us (45%)
  local copies, waits for them, and re-layouts  379 us (29%)
  matrix products  185 us (14%)
  blocking collectives  58.1 us (5%)
  other arithmetic  50.4 us (4%)
  between operations  21 us (2%)
    reduce_scatter x1, waiting for transfers between devices, shards(): lax.psum_scatter(grad_slots.astype(jnp.bfloat16), 'shard', scatter_dimens...  223 us
    all_gather x1, waiting for transfers between devices, shards(): lax.all_gather(tile_master.astype(jnp.bfloat16), 'shard', axis=0, tiled=T...  164 us
    psum x1, waiting for transfers between devices, shards(): lax.psum(own_tiles.astype(jnp.bfloat16), 'grp').astype(jnp.float32)  147 us
    unnamed x162, local copies, waits for them, and re-layouts  129 us
    reshape x5, local copies, waits for them, and re-layouts, untile(): block.reshape(row_count // tile_edge, col_count // tile_edge, tile_edge,...  70.8 us
    all_gather x1, waiting for transfers between devices, shards(): lax.all_gather(row_master.astype(jnp.bfloat16), 'shard', axis=1, tiled=True)  47.7 us
    psum x1, blocking collectives, shards(): whole_stats = lax.psum(statistics, ('grp', 'shard'))  43.5 us
    concatenate x1, local copies, waits for them, and re-layouts, shards(): dense_rows = jnp.concatenate([label_grad, rest_rows], axis=0)  41.3 us
  transfers between devices with their start and end apart: 5, of which 4 were waited for; matrix products, arithmetic and copies ran while one was open for 14% of the time, Pallas kernels for 0%

commit v1 on v0

v1 whole, which is shorter than its diff:
```python
import functools
import math

import jax
import jax.numpy as jnp
from jax import lax
from jax.experimental import pallas as pl
from jax.experimental.pallas import tpu as pltpu
from jax.sharding import PartitionSpec as P

D = 1024
HEADS = 16
HD = 64
FF = 4096
NCLASS = 1000
FREQ = 256
PATCH_SIDE = 2
LAT = 32
BLK = 256
PATCH_DIM = 16
SEQ = 256

NB = D // BLK
HB = FF // BLK
QB = 3 * NB
ADA = NB * 6 * NB
BIG = NB * QB + NB * NB + 2 * NB * HB
AT_QKV, AT_OUT, AT_UP, AT_DOWN = 0, NB * QB, NB * QB + NB * NB, NB * QB + NB * NB + NB * HB
L_ATT, L_OUT, L_MLP, L_HID = 0, NB, 2 * NB, 3 * NB
R_QKV = 3 * NB + HB
R_OUT = R_QKV + QB
R_UP = R_OUT + NB
R_DOWN = R_UP + HB
ACTS = R_DOWN + NB
B_OUT, B_UP, B_DOWN = QB, QB + NB, QB + NB + HB
ROW_STEP = 16
LANES = D // 128
NEAR = 64
NEAR_START = NCLASS + FREQ + 3 * D
N_PATCH, N_TIME1, N_TIME2, N_QUERY, N_VALUE, N_OUT, N_DOWN, N_ADA = range(2 * PATCH_DIM, 2 * PATCH_DIM + 8)
N_UP = N_ADA + 6
N_FINAL = N_UP + FF // D
NEAR_REAL = N_FINAL + 2
T_PATCH, T_OUT, T_DOWN, T_QUERY, T_VALUE, T_UP = range(2 * PATCH_DIM, 2 * PATCH_DIM + 6)
T_END = T_UP + FF // D
TOKEN_ROWS = 48

GROUPS, SHARDS = 4, 8
MESH_ID = pl.DeviceIdType.MESH

ln_eps = 1e-06
beta_one = 0.5
beta_two = 0.5
adam_eps = 1e-08
rate_step = 0.01
decay_rate = 0.1
clip_at = 0.25

f32 = jnp.float32
bf16 = jnp.bfloat16


def nn(left, right):
    return lax.dot_general(left, right, (((1,), (0,)), ((), ())), preferred_element_type=f32)


def nt(left, right):
    return lax.dot_general(left, right, (((1,), (1,)), ((), ())), preferred_element_type=f32)


def tn(left, right):
    return lax.dot_general(left, right, (((0,), (0,)), ((), ())), preferred_element_type=f32)


def wide(ref, at, count=ROW_STEP):
    return jnp.concatenate([ref[r, pl.ds(at, count), :] for r in range(NB)], axis=1)


def put(ref, base, at, value, count=ROW_STEP):
    for r in range(NB):
        ref[base + r, pl.ds(at, count), :] = value[:, r * BLK : (r + 1) * BLK].astype(ref.dtype)


def fold(value):
    return jnp.sum(value.reshape(-1, 8, value.shape[-1]), axis=0)


def normed(value):
    centred = value - jnp.mean(value, axis=-1, keepdims=True)
    spread = jnp.mean(centred * centred, axis=-1, keepdims=True)
    back = lax.rsqrt(spread + ln_eps)
    return centred * back, back


def over_rows(body):
    def step(i, unused):
        body(pl.multiple_of(i * ROW_STEP, ROW_STEP))
        return unused

    lax.fori_loop(0, SEQ // ROW_STEP, step, 0)


def over(count, body):
    def step(i, unused):
        body(i)
        return unused

    lax.fori_loop(0, count, step, 0)


def norm_back(grad, value, scale):
    norm, back = normed(value)
    inner = grad * (1.0 + scale)
    mean_one = jnp.mean(inner, axis=-1, keepdims=True)
    mean_two = jnp.mean(inner * norm, axis=-1, keepdims=True)
    return norm, (inner - mean_one - norm * mean_two) * back


def gelu_pair(value):
    root = math.sqrt(2.0 / math.pi)
    square = value * value
    bend = jnp.tanh(root * (value + 0.044715 * value * square))
    half = 0.5 * (1.0 + bend)
    slope = half + 0.5 * value * (1.0 - bend * bend) * root * (1.0 + 3 * 0.044715 * square)
    return value * half, slope


def block_body(
    loss_factor, place_ref, tiles_ref, patches_ref, noise_ref, spot_ref, near_ref, mods_ref,
    acts_ref, dmod_ref, ends_ref, stats_ref,
    w_ref, stream, middle, last, out_att, out_mlp, low_in, low_att, qkv, hid, slope, probs, flow, sums,
    near_wide, bias_ref, mod_ref, dbias_ref, w_sem,
):
    att_scale = HD ** (-0.5)
    cuts = (AT_QKV, AT_OUT, AT_UP, AT_DOWN, BIG)

    def fetch(b, sem):
        pltpu.make_async_copy(tiles_ref.at[place_ref[b]], w_ref.at[b], w_sem.at[sem]).start()

    for m in range(4):
        over(cuts[m + 1] - cuts[m], lambda b, m=m: fetch(cuts[m] + b, m))

    def arrived(m):
        span = pl.ds(cuts[m], cuts[m + 1] - cuts[m])
        pltpu.make_async_copy(tiles_ref.at[pl.ds(0, cuts[m + 1] - cuts[m])], w_ref.at[span], w_sem.at[m]).wait()

    def mod(i):
        return mod_ref[i : i + 1, :]

    near_wide[...] = near_ref[...].astype(f32)

    def row_block(row, r):
        return jnp.concatenate([near_wide[2 * r, row : row + 1, :], near_wide[2 * r + 1, row : row + 1, :]], axis=1)

    def near_block(row, r):
        span = slice(row, row + PATCH_DIM)
        return jnp.concatenate([near_ref[2 * r, span, :], near_ref[2 * r + 1, span, :]], axis=1)

    for r in range(NB):
        bias_ref[r] = row_block(N_QUERY, r)
        bias_ref[NB + r] = jnp.zeros((1, BLK), f32)
        bias_ref[2 * NB + r] = row_block(N_VALUE, r)
        bias_ref[B_OUT + r] = row_block(N_OUT, r)
        bias_ref[B_DOWN + r] = row_block(N_DOWN, r)
        for i in range(FF // D):
            bias_ref[B_UP + i * NB + r] = row_block(N_UP + i, r)
    for i in range(8):
        mod_ref[i : i + 1, :] = jnp.concatenate([mods_ref[i * LANES + o : i * LANES + o + 1, :] for o in range(LANES)], axis=1)

    lane = lax.broadcasted_iota(jnp.int32, (SEQ, 128), 1)
    lower = lane < HD
    halves = (lower, jnp.logical_not(lower))

    def masked(value, side):
        return jnp.where(halves[side], value, jnp.zeros_like(value))

    sums[...] = jnp.zeros_like(sums)
    S_SQ_END, S_SQ_ATT, S_SQ_MLP = 0, 1, 2
    S_DSH_A, S_DSC_A, S_DG_A, S_DSH_M, S_DSC_M, S_DG_M, S_DSH_F, S_DSC_F = range(3, 11)
    S_PATCH, S_OUT, S_DOWN = 11, 12, 13

    def collect(which, value):
        sums[which] = sums[which] + fold(value)

    patches = patches_ref[...]
    for r in range(NB):
        span = slice(r * BLK, (r + 1) * BLK)
        stream[r] = nn(patches, near_block(0, r)) + row_block(N_PATCH, r) + spot_ref[:, span]

    def modulate(source, scale, shift):
        def body(at):
            norm, _ = normed(wide(source, at))
            put(low_in, 0, at, norm * (1.0 + scale) + shift)

        over_rows(body)

    def transposed(base, ref, count):
        over(count, lambda r: acts_ref.__setitem__(base + r, ref[r].T))

    modulate(stream, mod(1), mod(0))
    transposed(L_ATT, low_in, NB)
    arrived(0)

    def qkv_step(c):
        total = nn(low_in[0], w_ref[AT_QKV + c])
        for r in range(1, NB):
            total += nn(low_in[r], w_ref[AT_QKV + r * QB + c])
        qkv[c] = (total + bias_ref[c]).astype(bf16)

    over(QB, qkv_step)

    def attend(c):
        for half in range(2):
            span = slice(half * 128, (half + 1) * 128)
            q, k, v = qkv[c, :, span], qkv[NB + c, :, span], qkv[2 * NB + c, :, span]
            parts = []
            for side in range(2):
                scores = nt(masked(q, side), k) * att_scale
                top = jnp.max(scores, axis=-1, keepdims=True)
                power = jnp.exp(scores - top)
                prob = power / jnp.sum(power, axis=-1, keepdims=True)
                probs[c * 4 + half * 2 + side] = prob
                parts.append(nn(prob.astype(bf16), v))
            low_att[c, :, span] = jnp.where(lower, parts[0], parts[1]).astype(bf16)

    over(NB, attend)
    transposed(L_OUT, low_att, NB)
    arrived(1)

    def out_step(c):
        total = nn(low_att[0], w_ref[AT_OUT + c])
        for r in range(1, NB):
            total += nn(low_att[r], w_ref[AT_OUT + r * NB + c])
        out_att[c] = total + bias_ref[B_OUT + c]

    over(NB, out_step)

    def mid_step(at):
        branch = mod(2) * wide(out_att, at)
        collect(S_SQ_ATT, branch * branch)
        value = wide(stream, at) + branch
        put(middle, 0, at, value)
        norm, _ = normed(value)
        put(low_in, 0, at, norm * (1.0 + mod(4)) + mod(3))

    over_rows(mid_step)
    transposed(L_MLP, low_in, NB)
    arrived(2)

    def up_step(c):
        total = nn(low_in[0], w_ref[AT_UP + c])
        for r in range(1, NB):
            total += nn(low_in[r], w_ref[AT_UP + r * HB + c])
        value, back = gelu_pair(total + bias_ref[B_UP + c])
        slope[c] = back
        low = value.astype(bf16)
        hid[c] = low
        acts_ref[L_HID + c] = low.T

    over(HB, up_step)
    arrived(3)

    def down_step(c):
        total = nn(hid[0], w_ref[AT_DOWN + c])
        for r in range(1, HB):
            total += nn(hid[r], w_ref[AT_DOWN + r * NB + c])
        out_mlp[c] = total + bias_ref[B_DOWN + c]

    over(NB, down_step)

    def end_step(at):
        branch = mod(5) * wide(out_mlp, at)
        collect(S_SQ_MLP, branch * branch)
        value = wide(middle, at) + branch
        collect(S_SQ_END, value * value)
        put(last, 0, at, value)
        norm, _ = normed(value)
        put(low_in, 0, at, norm * (1.0 + mod(7)) + mod(6))

    over_rows(end_step)
    predicted = nt(low_in[0], near_block(PATCH_DIM, 0))
    for r in range(1, NB):
        predicted += nt(low_in[r], near_block(PATCH_DIM, r))
    mismatch = predicted - noise_ref[...]
    loss_sum = jnp.sum(mismatch * mismatch)
    pred_low = (loss_factor * mismatch).astype(bf16)
    def put_rows(row, count, r, value):
        for i in range(2):
            ends_ref[2 * r + i, row : row + count, :] = value[:, i * 128 : (i + 1) * 128]

    for r in range(NB):
        put_rows(PATCH_DIM, PATCH_DIM, r, tn(pred_low, low_in[r]))
        flow[r] = nn(pred_low, near_block(PATCH_DIM, r))

    def end_back(at):
        grad = wide(flow, at)
        norm, value = norm_back(grad, wide(last, at), mod(7))
        collect(S_DSC_F, grad * norm)
        collect(S_DSH_F, grad)
        put(last, 0, at, value)
        collect(S_DG_M, value * wide(out_mlp, at))
        down = value * mod(5)
        collect(S_DOWN, down)
        put(acts_ref, R_DOWN, at, down)

    over_rows(end_back)

    def up_back(c):
        total = nt(acts_ref[R_DOWN], w_ref[AT_DOWN + c * NB])
        for j in range(1, NB):
            total += nt(acts_ref[R_DOWN + j], w_ref[AT_DOWN + c * NB + j])
        value = total * slope[c]
        dbias_ref[2 * NB + c] = jnp.sum(value, axis=0, keepdims=True)
        acts_ref[R_UP + c] = value.astype(bf16)

    over(HB, up_back)

    def mlp_back(r):
        total = nt(acts_ref[R_UP], w_ref[AT_UP + r * HB])
        for c in range(1, HB):
            total += nt(acts_ref[R_UP + c], w_ref[AT_UP + r * HB + c])
        flow[r] = total

    over(NB, mlp_back)

    def mid_back(at):
        grad = wide(flow, at)
        norm, value = norm_back(grad, wide(middle, at), mod(4))
        collect(S_DSC_M, grad * norm)
        collect(S_DSH_M, grad)
        value = value + wide(last, at)
        put(middle, 0, at, value)
        collect(S_DG_A, value * wide(out_att, at))
        proj = value * mod(2)
        collect(S_OUT, proj)
        put(acts_ref, R_OUT, at, proj)

    over_rows(mid_back)

    def att_back(r):
        total = nt(acts_ref[R_OUT], w_ref[AT_OUT + r * NB])
        for c in range(1, NB):
            total += nt(acts_ref[R_OUT + c], w_ref[AT_OUT + r * NB + c])
        low_att[r] = total.astype(bf16)

    over(NB, att_back)

    def attend_back(c):
        for half in range(2):
            span = slice(half * 128, (half + 1) * 128)
            q, k, v = qkv[c, :, span], qkv[NB + c, :, span], qkv[2 * NB + c, :, span]
            grad = low_att[c, :, span]
            found = []
            for side in range(2):
                prob = probs[c * 4 + half * 2 + side]
                dprob = nt(masked(grad, side), v)
                dvalue = tn(prob.astype(bf16), grad)
                dscore = prob * (dprob - jnp.sum(dprob * prob, axis=-1, keepdims=True))
                low = dscore.astype(bf16)
                found.append((nn(low, k) * att_scale, tn(low, q) * att_scale, dvalue))
            merged = [jnp.where(lower, one, two) for one, two in zip(*found)]
            for i in range(3):
                acts_ref[R_QKV + i * NB + c, :, span] = merged[i].astype(bf16)
            dbias_ref[c, :, span] = jnp.sum(merged[0], axis=0, keepdims=True)
            dbias_ref[NB + c, :, span] = jnp.sum(merged[2], axis=0, keepdims=True)

    over(NB, attend_back)

    def in_back(r):
        total = nt(acts_ref[R_QKV], w_ref[AT_QKV + r * QB])
        for c in range(1, QB):
            total += nt(acts_ref[R_QKV + c], w_ref[AT_QKV + r * QB + c])
        flow[r] = total

    over(NB, in_back)

    def first_back(at):
        grad = wide(flow, at)
        norm, value = norm_back(grad, wide(stream, at), mod(1))
        collect(S_DSC_A, grad * norm)
        collect(S_DSH_A, grad)
        value = value + wide(middle, at)
        collect(S_PATCH, value)
        put(low_in, 0, at, value)

    over_rows(first_back)
    for r in range(NB):
        put_rows(0, PATCH_DIM, r, tn(patches, low_in[r]))

    def total_of(which):
        return jnp.sum(sums[which], axis=0, keepdims=True)

    for i in range(8):
        value = total_of(S_DSH_A + i)
        for o in range(LANES):
            dmod_ref[i * LANES + o : i * LANES + o + 1, :] = value[:, o * 128 : (o + 1) * 128]
    for row, which in ((T_PATCH, S_PATCH), (T_OUT, S_OUT), (T_DOWN, S_DOWN)):
        value = total_of(which)
        for r in range(NB):
            put_rows(row, 1, r, value[:, r * BLK : (r + 1) * BLK])
    for r in range(NB):
        put_rows(T_QUERY, 1, r, dbias_ref[r])
        put_rows(T_VALUE, 1, r, dbias_ref[NB + r])
        for i in range(FF // D):
            put_rows(T_UP + i, 1, r, dbias_ref[2 * NB + i * NB + r])
    ends_ref[:, T_END:, :] = jnp.zeros((LANES, TOKEN_ROWS - T_END, 128), f32)
    row = lax.broadcasted_iota(jnp.int32, (8, 128), 0)
    found = jnp.where(row == 0, loss_sum, 0.0)
    for i in range(3):
        found = jnp.where(row == i + 1, jnp.sum(sums[i]), found)
    stats_ref[...] = found


def block_step(place, tiles, patches, noise, spots, near, mods, loss_factor):
    vmem = pl.BlockSpec(memory_space=pltpu.VMEM)
    macs = 3 * SEQ * BIG * BLK * BLK
    return pl.pallas_call(
        functools.partial(block_body, loss_factor),
        out_shape=[
            jax.ShapeDtypeStruct((ACTS, BLK, BLK), bf16),
            jax.ShapeDtypeStruct((8 * LANES, 128), f32),
            jax.ShapeDtypeStruct((LANES, TOKEN_ROWS, 128), f32),
            jax.ShapeDtypeStruct((8, 128), f32),
        ],
        in_specs=[pl.BlockSpec(memory_space=pltpu.SMEM), pl.BlockSpec(memory_space=pl.ANY)] + [vmem] * 5,
        out_specs=[vmem] * 4,
        scratch_shapes=[
            pltpu.VMEM((BIG, BLK, BLK), bf16),
            pltpu.VMEM((NB, SEQ, BLK), f32),
            pltpu.VMEM((NB, SEQ, BLK), f32),
            pltpu.VMEM((NB, SEQ, BLK), f32),
            pltpu.VMEM((NB, SEQ, BLK), f32),
            pltpu.VMEM((NB, SEQ, BLK), f32),
            pltpu.VMEM((NB, SEQ, BLK), bf16),
            pltpu.VMEM((NB, SEQ, BLK), bf16),
            pltpu.VMEM((QB, SEQ, BLK), bf16),
            pltpu.VMEM((HB, SEQ, BLK), bf16),
            pltpu.VMEM((HB, SEQ, BLK), f32),
            pltpu.VMEM((HEADS, SEQ, SEQ), f32),
            pltpu.VMEM((NB, SEQ, BLK), f32),
            pltpu.VMEM((14, 8, D), f32),
            pltpu.VMEM((LANES, NEAR, 128), f32),
            pltpu.VMEM((B_DOWN + NB, 1, BLK), f32),
            pltpu.VMEM((8, D), f32),
            pltpu.VMEM((2 * NB + HB, 1, BLK), f32),
            pltpu.SemaphoreType.DMA((4,)),
        ],
        compiler_params=pltpu.CompilerParams(vmem_limit_bytes=61 << 20),
        cost_estimate=pl.CostEstimate(flops=2 * macs, bytes_accessed=BIG * BLK * BLK * 4, transcendentals=0),
        name="block_step",
    )(place, tiles, patches, noise, spots, near, mods)


def ada_front_body(row_ref, col_ref, cond_ref, tile_ref, out_ref):
    s = pl.program_id(0)

    @pl.when(s == 0)
    def _():
        out_ref[...] = jnp.zeros_like(out_ref)

    @pl.when(col_ref[s] >= 0)
    def _():
        c = col_ref[s]
        out_ref[c] = out_ref[c] + nn(cond_ref[row_ref[s]], tile_ref[0].astype(bf16))


def ada_front(row_of, col_of, cond_blocks, tile_master):
    per, images = tile_master.shape[0], cond_blocks.shape[1]
    return pl.pallas_call(
        ada_front_body,
        grid_spec=pltpu.PrefetchScalarGridSpec(
            num_scalar_prefetch=2,
            grid=(per,),
            in_specs=[
                pl.BlockSpec(cond_blocks.shape, lambda s, r, c: (0, 0, 0)),
                pl.BlockSpec((1, BLK, BLK), lambda s, r, c: (s, 0, 0)),
            ],
            out_specs=pl.BlockSpec((6 * NB, images, BLK), lambda s, r, c: (0, 0, 0)),
        ),
        out_shape=jax.ShapeDtypeStruct((6 * NB, images, BLK), f32),
        name="ada_front",
    )(row_of, col_of, cond_blocks, tile_master)


def ada_back_body(row_ref, col_ref, dmod_ref, tile_ref, out_ref):
    s = pl.program_id(0)

    @pl.when(s == 0)
    def _():
        out_ref[...] = jnp.zeros_like(out_ref)

    @pl.when(col_ref[s] >= 0)
    def _():
        r = row_ref[s]
        out_ref[r] = out_ref[r] + nt(dmod_ref[col_ref[s]], tile_ref[0].astype(bf16))


def ada_back(row_of, col_of, dmod_blocks, tile_master):
    per, images = tile_master.shape[0], dmod_blocks.shape[1]
    return pl.pallas_call(
        ada_back_body,
        grid_spec=pltpu.PrefetchScalarGridSpec(
            num_scalar_prefetch=2,
            grid=(per,),
            in_specs=[
                pl.BlockSpec(dmod_blocks.shape, lambda s, r, c: (0, 0, 0)),
                pl.BlockSpec((1, BLK, BLK), lambda s, r, c: (s, 0, 0)),
            ],
            out_specs=pl.BlockSpec((NB, images, BLK), lambda s, r, c: (0, 0, 0)),
        ),
        out_shape=jax.ShapeDtypeStruct((NB, images, BLK), f32),
        name="ada_back",
    )(row_of, col_of, dmod_blocks, tile_master)


def tile_grad_body(left_ref, right_ref, acts_ref, out_ref):
    s = pl.program_id(0)
    out_ref[0] = nn(acts_ref[left_ref[s]], acts_ref[right_ref[s]]).astype(bf16)


def tile_grads(left_of, right_of, acts):
    count = left_of.shape[0]
    return pl.pallas_call(
        tile_grad_body,
        grid_spec=pltpu.PrefetchScalarGridSpec(
            num_scalar_prefetch=2,
            grid=(count,),
            in_specs=[pl.BlockSpec(acts.shape, lambda s, a, b: (0, 0, 0))],
            out_specs=pl.BlockSpec((1, BLK, BLK), lambda s, a, b: (s, 0, 0)),
        ),
        out_shape=jax.ShapeDtypeStruct((count, BLK, BLK), bf16),
        compiler_params=pltpu.CompilerParams(vmem_limit_bytes=40 << 20),
        name="tile_grads",
    )(left_of, right_of, acts)


def adam_body(group, where_ref, row_ref, col_ref, factor_ref, grads_ref, cond_ref, dmod_ref, bases_ref, moment_ref, second_ref,
              new_moment_ref, new_second_ref, update_ref, grad):
    step = pl.program_id(0)
    factor = factor_ref[0]
    for j in range(group):
        s = step * group + j

        @pl.when(col_ref[s] >= 0)
        def _():
            grad[...] = nn(cond_ref[row_ref[s]], dmod_ref[jnp.maximum(col_ref[s], 0)]).astype(bf16)

        @pl.when(col_ref[s] < 0)
        def _():
            grad[...] = grads_ref[where_ref[s]]

        left, right = bases_ref[j, 0].astype(bf16), bases_ref[j, 1].astype(bf16)
        turned = factor * nn(left.T, nn(grad[...], right).astype(bf16))
        moment = beta_one * moment_ref[j] + (1.0 - beta_one) * turned
        second = beta_two * second_ref[j] + (1.0 - beta_two) * turned * turned
        new_moment_ref[j] = moment
        new_second_ref[j] = second
        direction = (moment / (jnp.sqrt(second) + adam_eps)).astype(bf16)
        update_ref[j] = -rate_step * nt(nn(left, direction).astype(bf16), right)


def adam(where, row_of, col_of, factor, grads, cond_blocks, dmod_blocks, bases, moment, second):
    per = moment.shape[0]
    group = next(g for g in (3, 2, 1) if per % g == 0)
    tile = pl.BlockSpec((group, BLK, BLK), lambda s, *_: (s, 0, 0))

    def whole(array):
        return pl.BlockSpec(array.shape, lambda s, *_: (0,) * array.ndim)

    shape = jax.ShapeDtypeStruct(moment.shape, f32)
    return pl.pallas_call(
        functools.partial(adam_body, group),
        grid_spec=pltpu.PrefetchScalarGridSpec(
            num_scalar_prefetch=4,
            grid=(per // group,),
            in_specs=[
                whole(grads),
                whole(cond_blocks),
                whole(dmod_blocks),
                pl.BlockSpec((group, 2, BLK, BLK), lambda s, *_: (s, 0, 0, 0)),
                tile,
                tile,
            ],
            out_specs=[tile] * 3,
            scratch_shapes=[pltpu.VMEM((BLK, BLK), bf16)],
        ),
        out_shape=[shape] * 3,
        compiler_params=pltpu.CompilerParams(vmem_limit_bytes=56 << 20),
        name="adam_tiles",
    )(where, row_of, col_of, factor, grads, cond_blocks, dmod_blocks, bases, moment, second)

def spread_body(
    cap, n_third,
    slot_ref, row_ref, col_ref, tiles_ref, rows_ref, ids_ref,
    out_ref, near_ref, mods_ref, freq_ref, label_ref, time_ref, cond_ref, pre_ref, own_cond_ref,
    tile, pack, ids, near, times, conds, near_wide, cond_group, product, part, part_out, part_in,
    load_sem, keep_sem, send_sem, recv_sem, small_send, small_recv,
):
    z, s = lax.axis_index("grp"), lax.axis_index("shard")
    per = tile.shape[0]
    images = GROUPS * SHARDS
    third = cap // 3
    step = third // n_third
    x_at, y_at, c_at, z_at = (z, s ^ 2), (z, s ^ 4), (z, s ^ 1), (z ^ 1, s)
    far_z = [(lax.rem(z + i, GROUPS), s) for i in range(1, GROUPS)]
    near_s = [(z, s ^ i) for i in range(1, SHARDS)]

    barrier = pltpu.get_barrier_semaphore()
    for peer in far_z + near_s:
        pl.semaphore_signal(barrier, inc=1, device_id=peer, device_id_type=MESH_ID)
    load = pltpu.make_async_copy(tiles_ref, tile, load_sem)
    load.start()

    def block_rows(index, count):
        return pl.ds(pl.multiple_of(index * count, count), count)

    ids[block_rows(s * GROUPS + z, 8), :] = ids_ref[...]
    near_wide[...] = jnp.zeros_like(near_wide)
    near_wide[: NEAR_REAL - 3, :] = rows_ref[NEAR_START : NEAR_START + NEAR_REAL - 3, :]
    near_wide[NEAR_REAL - 3 : NEAR_REAL, :] = rows_ref[NEAR_START + NEAR_REAL - 3 : NEAR_START + NEAR_REAL, :]
    near[s] = near_wide[...].astype(bf16)
    near_wide[...] = near_wide[...].astype(bf16).astype(f32)
    pl.semaphore_wait(barrier, len(far_z) + len(near_s))

    sent = []

    def push(src, dst, peer, index):
        copy = pltpu.make_async_remote_copy(
            src_ref=src, dst_ref=dst, send_sem=small_send.at[index], recv_sem=small_recv.at[index],
            device_id=peer, device_id_type=MESH_ID,
        )
        copy.start()
        sent.append(copy)
        return copy

    def to_group(stage, pairs):
        first = len(far_z) + stage * len(near_s)
        return [push(*pairs(peer[1]), peer, first + i) for i, peer in enumerate(near_s)]

    def got(copies):
        for copy in copies:
            copy.wait_recv()

    own_ids = ids.at[block_rows(s * GROUPS + z, 8)]
    id_far = [push(own_ids, own_ids, peer, i) for i, peer in enumerate(far_z)]
    near_copies = to_group(0, lambda p: (near.at[s], near.at[s]))

    parity = lax.rem(z, 2)
    starts = (third + parity * third, 0, 2 * third - parity * third)

    def chunk(index):
        kind, at = divmod(index, n_third)
        return pl.ds(starts[kind] + at * step, step)

    load.wait()
    big = []

    def send(kind, stream, index, peer, src, owner, arrives):
        copy = pltpu.make_async_remote_copy(
            src_ref=src, dst_ref=out_ref.at[owner, chunk(index)],
            send_sem=send_sem.at[kind, index], recv_sem=recv_sem.at[stream, arrives],
            device_id=peer, device_id_type=MESH_ID,
        )
        copy.start()
        big.append(copy)

    def wait_for(stream, index, owner):
        place = out_ref.at[owner, chunk(index)]
        pltpu.make_async_remote_copy(
            src_ref=place, dst_ref=place, send_sem=send_sem.at[0, index], recv_sem=recv_sem.at[stream, index],
            device_id=x_at, device_id_type=MESH_ID,
        ).wait_recv()

    def pack_chunk(index):
        kind, at = divmod(index, n_third)

        def one(i, unused):
            p = starts[kind] + at * step + i
            pack[p] = tile[slot_ref[p]].astype(bf16)
            return unused

        lax.fori_loop(0, step, one, 0)

    def send_mine(index):
        src = pack.at[chunk(index)]
        if index < 2 * n_third:
            send(0, 0, index, x_at, src, s, index)
            send(1, 1, index, y_at, src, s, index)
        send(2, 3, index, c_at, src, s, index)

    owners = (s ^ 2, s ^ 4, s ^ 6)

    def pass_on(which, index):
        owner = owners[which]
        wait_for(which, index, owner)
        here = out_ref.at[owner, chunk(index)]
        if index < 2 * n_third:
            if which == 0 and index % 2 == 0:
                send(6, 2, index, y_at, here, owner, index)
            if which == 1 and index % 2 == 1:
                send(7, 2, index, x_at, here, owner, index)
        if index < n_third:
            send(8 + which, which, index, z_at, here, owner, 2 * n_third + index)
        send(3 + which, 4 + which, index, c_at, here, owner, index)

    for j in range(n_third):
        pack_chunk(j)
        send_mine(j)
    got(id_far)
    span = block_rows(s, 8 * GROUPS)
    id_near = to_group(1, lambda p: (ids.at[span], ids.at[span]))
    for j in range(n_third, 3 * n_third):
        pack_chunk(j)
    keep = pltpu.make_async_copy(pack, out_ref.at[s, pl.ds(0, cap)], keep_sem)
    keep.start()
    stages = {}

    def silu_low(value):
        return (value * jax.nn.sigmoid(value)).astype(bf16)

    def row_slice(start, count):
        return rows_ref[start : start + count, :].astype(bf16)

    def time_stage():
        got(id_near)
        freq = jnp.concatenate([ids[pl.ds(i, images, stride=8), :] for i in range(2)], axis=1).astype(bf16)
        freq_ref[...] = freq
        label_ref[...] = ids[pl.ds(2, images, stride=8), :]
        pre = nn(freq, row_slice(NCLASS, FREQ)) + near_wide[N_TIME1 : N_TIME1 + 1, :]
        pre_ref[...] = pre
        times[s] = silu_low(pre)
        stages["time"] = to_group(2, lambda p: (times.at[s], times.at[s]))

    def cond_stage():
        got(stages["time"])
        total = jnp.zeros((images, 128), f32) + near_wide[N_TIME2 : N_TIME2 + 1, :]
        for o in range(SHARDS):
            total += nn(times[o], row_slice(NCLASS + FREQ + o * 128, 128))
        hot = label_ref[...].astype(jnp.int32)[:, :1] == lax.broadcasted_iota(jnp.int32, (images, D), 1)
        total += nn(hot.astype(bf16), row_slice(0, D))
        own_cond_ref[...] = total
        conds[s] = silu_low(total)
        stages["cond"] = to_group(3, lambda p: (conds.at[s], conds.at[s]))

    def group_stage():
        got(stages["cond"])
        at = lax.broadcasted_iota(jnp.int32, (SHARDS, images), 1)
        row = lax.broadcasted_iota(jnp.int32, (SHARDS, images), 0)
        pick = (at == row * GROUPS + z).astype(bf16)
        for o in range(SHARDS):
            half = o % 2
            cond_group[o // 2, :, half * 128 : (half + 1) * 128] = nn(pick, conds[o])

    def ada_stage(start, count):
        def one(j, unused):
            product[start + j] = nn(cond_group[row_ref[start + j]].astype(bf16), tile[start + j].astype(bf16))
            return unused

        lax.fori_loop(0, count, one, 0)

    def part_stage():
        part[...] = jnp.zeros_like(part)

        def column(c, unused):
            total = jnp.zeros((SHARDS, BLK), f32)
            for j in range(per):
                total += jnp.where(col_ref[j] == c, 1.0, 0.0) * product[j]
            for half in range(2):
                part[block_rows(2 * c + half, 8), :] = total[:, half * 128 : (half + 1) * 128]
            return unused

        lax.fori_loop(0, 6 * NB, column, 0)
        for i in range(6):
            place = block_rows(i * LANES + s, 8)
            part[place, :] = part[place, :] + near_wide[N_ADA + i : N_ADA + i + 1, :]
        for i in range(2):
            total = jnp.zeros((SHARDS, 128), f32) + near_wide[N_FINAL + i : N_FINAL + i + 1, :]
            for r in range(NB):
                weight = row_slice(NCLASS + FREQ + D + i * D + r * BLK, BLK)
                total += nn(cond_group[r].astype(bf16), weight)
            part[block_rows((6 + i) * LANES + s, 8), :] = total
        for o in range(SHARDS):
            part_out[o] = part[pl.ds(o, 8 * LANES, stride=8), :]
        part_in[s] = part_out[s]
        stages["part"] = to_group(4, lambda p: (part_out.at[p], part_in.at[s]))

    def mod_stage():
        got(stages["part"])
        total = part_in[0]
        for o in range(1, SHARDS):
            total += part_in[o]
        mods_ref[...] = total
        got(near_copies)
        near_ref[...] = near[...]
        time_ref[...] = times[...]
        cond_ref[...] = conds[...]

    cut = per // 3
    hooks = [
        time_stage, cond_stage, group_stage, lambda: ada_stage(0, cut), lambda: ada_stage(cut, cut),
        lambda: ada_stage(2 * cut, per - 2 * cut), part_stage, mod_stage,
    ]
    seen = [0]

    def hook():
        if hooks:
            hooks.pop(0)()

    def z_next():
        order = [(w, 2 * n_third + j) for j in range(n_third) for w in (0, 1)]
        order += [(2, 2 * n_third + j) for j in range(n_third)]
        if seen[0] < len(order):
            pass_on(*order[seen[0]])
            seen[0] += 1

    for j in range(n_third):
        pass_on(0, j)
        pass_on(1, j)
        hook()
        if j:
            z_next()
    for j in range(n_third, 3 * n_third):
        send_mine(j)
    for j in range(n_third):
        pass_on(2, j)
        if j % 2:
            z_next()
            hook()
    for j in range(n_third, 2 * n_third):
        pass_on(0, j)
        pass_on(1, j)
        hook()
        z_next()
    for j in range(n_third, 2 * n_third):
        pass_on(2, j)
        if j % 2:
            z_next()
            hook()
    while hooks:
        hook()
    while seen[0] < 3 * n_third:
        z_next()
    for index in range(3 * n_third):
        wait_for(3, index, s ^ 1)
        for which in range(3):
            wait_for(4 + which, index, owners[which] ^ 1)
    keep.wait()
    for copy in big + sent:
        copy.wait_send()


def spread(cap, slot_of, row_of, col_of, tile_master, row_master, ids):
    per = tile_master.shape[0]
    n_third = 4 if cap // 3 % 4 == 0 else next(n for n in (5, 3, 2, 1) if cap // 3 % n == 0)
    images = GROUPS * SHARDS
    vmem = pl.BlockSpec(memory_space=pltpu.VMEM)
    smem = pl.BlockSpec(memory_space=pltpu.SMEM)
    anywhere = pl.BlockSpec(memory_space=pl.ANY)
    small = (GROUPS - 1) + 5 * (SHARDS - 1)
    return pl.pallas_call(
        functools.partial(spread_body, cap, n_third),
        out_shape=[
            jax.ShapeDtypeStruct((SHARDS, per, BLK, BLK), bf16),
            jax.ShapeDtypeStruct((LANES, NEAR, 128), bf16),
            jax.ShapeDtypeStruct((8 * LANES, 128), f32),
            jax.ShapeDtypeStruct((images, FREQ), bf16),
            jax.ShapeDtypeStruct((images, 128), f32),
            jax.ShapeDtypeStruct((SHARDS, images, 128), bf16),
            jax.ShapeDtypeStruct((SHARDS, images, 128), bf16),
            jax.ShapeDtypeStruct((images, 128), f32),
            jax.ShapeDtypeStruct((images, 128), f32),
        ],
        in_specs=[smem] * 3 + [anywhere] + [vmem] * 2,
        out_specs=[anywhere] + [vmem] * 8,
        scratch_shapes=[
            pltpu.VMEM((per, BLK, BLK), f32),
            pltpu.VMEM((cap, BLK, BLK), bf16),
            pltpu.VMEM((images * 8, 128), f32),
            pltpu.VMEM((LANES, NEAR, 128), bf16),
            pltpu.VMEM((SHARDS, images, 128), bf16),
            pltpu.VMEM((SHARDS, images, 128), bf16),
            pltpu.VMEM((NEAR, 128), f32),
            pltpu.VMEM((NB, SHARDS, BLK), f32),
            pltpu.VMEM((per, SHARDS, BLK), f32),
            pltpu.VMEM((8 * LANES * 8, 128), f32),
            pltpu.VMEM((SHARDS, 8 * LANES, 128), f32),
            pltpu.VMEM((SHARDS, 8 * LANES, 128), f32),
            pltpu.SemaphoreType.DMA,
            pltpu.SemaphoreType.DMA,
            pltpu.SemaphoreType.DMA((11, 3 * n_third)),
            pltpu.SemaphoreType.DMA((7, 3 * n_third)),
            pltpu.SemaphoreType.DMA((small,)),
            pltpu.SemaphoreType.DMA((small,)),
        ],
        compiler_params=pltpu.CompilerParams(collective_id=cap, has_side_effects=True, vmem_limit_bytes=40 << 20),
        name="spread",
    )(slot_of, row_of, col_of, tile_master, row_master, ids)

RING = 4
Z_LAG = 5


def collect_body(
    cap, ch,
    left_ref, right_ref, row_ref, col_ref, count_ref,
    acts_ref, dmod_ref, ends_ref, stats_ref, time_ref, cond_ref, freq_ref, label_ref, pre_ref, own_cond_ref, rows_ref, tiles_ref,
    grads_ref, d_blocks_ref, own_rows_ref, norm_ref, stat_ref,
    out_c, in_c, out_d, out_x, out_y, in_dx, in_dy, in_x, in_y, total, low_in, high_in, final,
    tile, product, all_d, wide_d, all_stats, tok_in, tok_z, tokens, part_out, part_in, pre_out, pre_in, own_dcond, own_dpre,
    vectors, squares, square_in,
    c_send, c_recv, d_send, dx_recv, dy_recv, x_send, x_recv, y_send, y_recv, up_send, low_recv, high_recv, final_recv, down_send,
    keep_sem, load_sem, small_send, small_recv,
):
    z, s = lax.axis_index("grp"), lax.axis_index("shard")
    per = product.shape[0]
    images = GROUPS * SHARDS
    chunks = cap // ch
    x_at, y_at, c_at = (z, s ^ 2), (z, s ^ 4), (z, s ^ 1)
    far_z = [(lax.rem(z + i, GROUPS), s) for i in range(1, GROUPS)]
    near_s = [(z, s ^ i) for i in range(1, SHARDS)]
    half = BLK // 2
    upper, lower = pl.ds(0, half), pl.ds(half, half)

    barrier = pltpu.get_barrier_semaphore()
    for peer in far_z + near_s:
        pl.semaphore_signal(barrier, inc=1, device_id=peer, device_id_type=MESH_ID)

    def remote(src, dst, sent, received, peer):
        return pltpu.make_async_remote_copy(
            src_ref=src, dst_ref=dst, send_sem=sent, recv_sem=received, device_id=peer, device_id_type=MESH_ID
        )

    def block_rows(index, count):
        return pl.ds(pl.multiple_of(index * count, count), count)

    def far(stage, src, dst):
        return [
            remote(src, dst, small_send.at[stage * 3 + i], small_recv.at[stage * 3 + i], peer) for i, peer in enumerate(far_z)
        ]

    def group(stage, src_of, dst):
        first = 9 + stage * 7
        return [
            remote(src_of(peer[1]), dst, small_send.at[first + i], small_recv.at[first + i], peer)
            for i, peer in enumerate(near_s)
        ]

    own_d = all_d.at[block_rows(s * GROUPS + z, 8 * LANES)]
    own_stat = all_stats.at[block_rows(s * GROUPS + z, 8)]
    group_d = all_d.at[block_rows(s, 8 * LANES * GROUPS)]
    group_stat = all_stats.at[block_rows(s, 8 * GROUPS)]

    def small_copies(name):
        if name == "d_far":
            return far(0, own_d, own_d)
        if name == "stat_far":
            return far(1, own_stat, own_stat)
        if name == "tok_far":
            return far(2, tok_z.at[z], tok_z.at[z])
        if name == "tok":
            return group(0, lambda p: ends_ref.at[p], tok_in.at[s])
        if name == "d":
            return group(1, lambda p: group_d, group_d)
        if name == "stat":
            return group(2, lambda p: group_stat, group_stat)
        if name == "part":
            return group(3, lambda p: part_out.at[p], part_in.at[s])
        if name == "pre":
            return group(4, lambda p: pre_out.at[p], pre_in.at[s])
        return group(5, lambda p: square_in.at[s], square_in.at[s])

    def begin(*names):
        for name in names:
            for copy in small_copies(name):
                copy.start()

    def got(*names):
        for name in names:
            for copy in small_copies(name):
                copy.wait_recv()

    def load(part):
        count = tile.shape[0]
        return pltpu.make_async_copy(tiles_ref.at[pl.ds(part * count, count)], tile, load_sem)

    load(0).start()
    own_d[...] = dmod_ref[...].astype(bf16)
    own_stat[...] = stats_ref[...]
    tok_in[s] = ends_ref[s]
    squares[...] = jnp.zeros_like(squares)
    pl.semaphore_wait(barrier, len(far_z) + len(near_s))
    begin("d_far", "stat_far", "tok")

    def spread_stage():
        got("d_far", "stat_far")
        begin("d", "stat")
        got("tok")
        value = tok_in[0]
        for o in range(1, SHARDS):
            value += tok_in[o]
        tok_z[z] = value
        begin("tok_far")

    def order_stage():
        got("d", "stat", "tok_far")
        value = tok_z[0]
        for i in range(1, GROUPS):
            value += tok_z[i]
        tokens[...] = value
        value = all_stats[pl.ds(0, 8), :]
        for i in range(1, images):
            value += all_stats[pl.ds(8 * i, 8), :]
        stat_ref[...] = value

        def widen(i, unused):
            place = block_rows(i, 8 * LANES)
            wide_d[place, :] = all_d[place, :].astype(f32)
            return unused

        lax.fori_loop(0, images, widen, 0)
        for q in range(6 * LANES):
            d_blocks_ref[q // 2, :, (q % 2) * 128 : (q % 2 + 1) * 128] = wide_d[
                pl.ds(q, images, stride=8 * LANES), :
            ].astype(bf16)

    def own_columns(i):
        return wide_d[pl.ds(i * LANES + s, images, stride=8 * LANES), :]

    def ada_stage(part):
        count = tile.shape[0]
        load(part).wait()

        def one(j, unused):
            at = part * count + j
            product[at] = nt(d_blocks_ref[jnp.maximum(col_ref[at], 0)], tile[j].astype(bf16))
            return unused

        lax.fori_loop(0, count, one, 0)
        if (part + 1) * count < per:
            load(part + 1).start()

    def row_slice(start, count):
        return rows_ref[start : start + count, :].astype(bf16)

    final_at = NCLASS + FREQ + D

    def part_stage():
        for r in range(NB):
            value = jnp.zeros((images, BLK), f32)
            for i in range(2):
                value += nt(own_columns(6 + i).astype(bf16), row_slice(final_at + i * D + r * BLK, BLK))

            def add(j, value, r=r):
                chosen = jnp.logical_and(col_ref[j] >= 0, row_ref[j] == r)
                return value + jnp.where(chosen, 1.0, 0.0) * product[j]

            value = lax.fori_loop(0, per, add, value)
            for i in range(2):
                part_out[2 * r + i] = value[:, i * 128 : (i + 1) * 128]
        part_in[s] = part_out[s]
        begin("part")

    def slope(value):
        gate = jax.nn.sigmoid(value)
        return gate * (1.0 + value * (1.0 - gate))

    def cond_stage():
        got("part")
        value = part_in[0]
        for o in range(1, SHARDS):
            value += part_in[o]
        value = value * slope(own_cond_ref[...])
        own_dcond[...] = value
        for o in range(SHARDS):
            pre_out[o] = nt(value.astype(bf16), row_slice(NCLASS + FREQ + o * 128, 128))
        pre_in[s] = pre_out[s]
        begin("pre")

    def row_stage():
        got("pre")
        value = pre_in[0]
        for o in range(1, SHARDS):
            value += pre_in[o]
        value = value * slope(pre_ref[...])
        own_dpre[...] = value
        dpre_low, dcond = value.astype(bf16), own_dcond[...]
        dcond_low = dcond.astype(bf16)
        gathered = []

        def keep(start, value):
            own_rows_ref[start : start + value.shape[0], :] = value
            gathered.append(fold(value * value))

        hot = label_ref[...].astype(jnp.int32)[:, :1] == lax.broadcasted_iota(jnp.int32, (images, NCLASS), 1)
        keep(
            0,
            lax.dot_general(
                hot.astype(f32), dcond, (((0,), (0,)), ((), ())), preferred_element_type=f32, precision=lax.Precision.HIGHEST
            ),
        )
        keep(NCLASS, tn(freq_ref[...], dpre_low))
        for o in range(SHARDS):
            keep(NCLASS + FREQ + o * 128, tn(time_ref[o], dcond_low))
            for i in range(2):
                keep(final_at + i * D + o * 128, tn(cond_ref[o], own_columns(6 + i).astype(bf16)))
        keep(NEAR_START, tokens[: 2 * PATCH_DIM, :])

        vectors[...] = jnp.zeros_like(vectors)

        def vector(row, value):
            vectors[row : row + 1, :] = value

        vector(0, tokens[T_PATCH : T_PATCH + 1, :])
        vector(1, jnp.sum(value, axis=0, keepdims=True))
        vector(2, jnp.sum(dcond, axis=0, keepdims=True))
        vector(3, tokens[T_QUERY : T_QUERY + 1, :])
        vector(4, tokens[T_VALUE : T_VALUE + 1, :])
        vector(5, tokens[T_OUT : T_OUT + 1, :])
        vector(6, tokens[T_DOWN : T_DOWN + 1, :])
        for i in range(8):
            vector(7 + i if i < 6 else 7 + i + FF // D, jnp.sum(own_columns(i), axis=0, keepdims=True))
        for i in range(FF // D):
            vector(13 + i, tokens[T_UP + i : T_UP + i + 1, :])
        start = NEAR_START + 2 * PATCH_DIM
        rest = own_rows_ref.shape[0] - start
        whole = rest // 8 * 8
        own_rows_ref[start : start + whole, :] = vectors[:whole, :]
        own_rows_ref[start + whole : start + rest, :] = vectors[whole:rest, :]
        value = fold(vectors[...] * vectors[...])
        for piece in gathered:
            value += piece
        squares[:, :128] = squares[:, :128] + value

    def slot_of(i):
        return lax.rem(i + RING, RING)

    def block(owner, p):
        at = owner * per + p
        return nn(acts_ref[left_ref[at]], acts_ref[right_ref[at]])

    targets = (s ^ 6, s ^ 2, s ^ 4, s)

    def c_copy(slot, item):
        return remote(out_c.at[slot, item], in_c.at[slot, item], c_send.at[slot, item], c_recv.at[slot, item], c_at)

    def dx_copy(slot):
        return remote(out_d.at[slot, :, upper], in_dx.at[slot], d_send.at[slot, 0], dx_recv.at[slot], x_at)

    def dy_copy(slot):
        return remote(out_d.at[slot, :, lower], in_dy.at[slot], d_send.at[slot, 1], dy_recv.at[slot], y_at)

    def x_copy(slot):
        return remote(out_x.at[slot], in_x.at[slot], x_send.at[slot], x_recv.at[slot], x_at)

    def y_copy(slot):
        return remote(out_y.at[slot], in_y.at[slot], y_send.at[slot], y_recv.at[slot], y_at)

    def inside(i):
        return jnp.logical_and(i >= 0, i < chunks)

    def each(body):
        def one(c, unused):
            body(c)
            return unused

        lax.fori_loop(0, ch, one, 0)

    def for_sibling(n):
        slot = slot_of(n)
        for item in range(4):
            at = n + 1 if item == 0 else n

            @pl.when(inside(at))
            def _():
                def one(c):
                    out_c[slot, item, c] = block(targets[item] ^ 1, at * ch + c).astype(bf16)

                each(one)
                c_copy(slot, item).start()

    def for_owners(i):
        slot, before = slot_of(i), slot_of(i - 1)

        @pl.when(inside(i + 1))
        def _():
            c_copy(slot, 0).wait_recv()

            def one(c):
                value = block(targets[0], (i + 1) * ch + c) + in_c[slot, 0, c].astype(f32)
                out_d[slot, c] = value.astype(bf16)

            each(one)
            dx_copy(slot).start()
            dy_copy(slot).start()

        @pl.when(inside(i))
        def _():
            c_copy(slot, 1).wait_recv()
            dy_copy(before).wait_recv()

            def one(c):
                value = block(targets[1], i * ch + c) + in_c[slot, 1, c].astype(f32)
                out_x[slot, c, upper] = value[:half].astype(bf16)
                out_x[slot, c, lower] = (value[half:] + in_dy[before, c].astype(f32)).astype(bf16)

            each(one)
            x_copy(slot).start()
            c_copy(slot, 2).wait_recv()
            dx_copy(before).wait_recv()

            def two(c):
                value = block(targets[2], i * ch + c) + in_c[slot, 2, c].astype(f32)
                out_y[slot, c, upper] = (value[:half] + in_dx[before, c].astype(f32)).astype(bf16)
                out_y[slot, c, lower] = value[half:].astype(bf16)

            each(two)
            y_copy(slot).start()
            c_copy(slot, 3).wait_recv()

            def three(c):
                value = block(targets[3], i * ch + c) + in_c[slot, 3, c].astype(f32)
                total[i * ch + c] = value.astype(bf16)

            each(three)

        @pl.when(inside(i - 1))
        def _():
            x_copy(before).wait_recv()
            y_copy(before).wait_recv()

            def one(c):
                at = (i - 1) * ch + c
                value = total[at].astype(f32) + in_x[before, c].astype(f32) + in_y[before, c].astype(f32)
                total[at] = value.astype(bf16)

            each(one)

    def along(j):
        even = lax.rem(j, 2) == 0
        rank = jnp.where(even, z, GROUPS - 1 - z)
        down = jnp.where(even, lax.rem(z + GROUPS - 1, GROUPS), lax.rem(z + 1, GROUPS))
        up = jnp.where(even, lax.rem(z + 1, GROUPS), lax.rem(z + GROUPS - 1, GROUPS))
        return rank, (down, s), (up, s)

    def z_copy(name, j):
        _, down, up = along(j)
        span = pl.ds(j * ch, ch)
        if name == "rise":
            return remote(total.at[span], low_in.at[span], up_send.at[j], low_recv.at[j], up)
        if name == "sink":
            return remote(total.at[span], high_in.at[span], up_send.at[j], high_recv.at[j], down)
        if name == "final_down":
            return remote(final.at[span], final.at[span], down_send.at[0, j], final_recv.at[j], down)
        return remote(final.at[span], final.at[span], down_send.at[1, j], final_recv.at[j], up)

    def over_z(i):
        j = i - 1

        @pl.when(inside(j))
        def _():
            rank, _, _ = along(j)

            @pl.when(rank == 0)
            def _():
                z_copy("rise", j).start()

            @pl.when(rank == 3)
            def _():
                z_copy("sink", j).start()

        j2 = i - 2

        @pl.when(jnp.logical_and(inside(j2), along(j2)[0] == 2))
        def _():
            z_copy("sink", j2).wait_recv()

            def one(c):
                at = j2 * ch + c
                total[at] = (total[at].astype(f32) + high_in[at].astype(f32)).astype(bf16)

            each(one)
            z_copy("sink", j2).start()

        j3 = i - 3

        @pl.when(jnp.logical_and(inside(j3), along(j3)[0] == 1))
        def _():
            z_copy("rise", j3).wait_recv()
            z_copy("sink", j3).wait_recv()

            def one(c):
                at = j3 * ch + c
                value = total[at].astype(f32) + low_in[at].astype(f32) + high_in[at].astype(f32)
                final[at] = value.astype(bf16)

            each(one)
            z_copy("final_down", j3).start()
            z_copy("final_up", j3).start()

        j4 = i - 4

        @pl.when(jnp.logical_and(inside(j4), along(j4)[0] == 2))
        def _():
            z_copy("final_up", j4).wait_recv()
            z_copy("final_up", j4).start()

        j5 = i - Z_LAG

        @pl.when(inside(j5))
        def _():
            rank = along(j5)[0]

            @pl.when(jnp.logical_or(rank == 0, rank == 3))
            def _():
                z_copy("final_up", j5).wait_recv()

            span = pl.ds(j5 * ch, ch)
            pltpu.make_async_copy(final.at[span], grads_ref.at[span], keep_sem.at[j5]).start()

            def one(c):
                at = j5 * ch + c
                value = final[at].astype(f32) * jnp.where(at < count_ref[0], 1.0, 0.0)
                squares[...] = squares[...] + fold(value * value)

            each(one)

    def settle(i):
        n = i - 1
        slot = slot_of(n)
        for item in range(4):

            @pl.when(inside(n + 1 if item == 0 else n))
            def _():
                c_copy(slot, item).wait_send()

        n2 = i - 2
        slot2 = slot_of(n2)

        @pl.when(inside(n2 + 1))
        def _():
            dx_copy(slot2).wait_send()
            dy_copy(slot2).wait_send()

        @pl.when(inside(n2))
        def _():
            x_copy(slot2).wait_send()
            y_copy(slot2).wait_send()

    hooks = {
        0: spread_stage, 2: order_stage, 3: lambda: ada_stage(0), 4: lambda: ada_stage(1), 5: lambda: ada_stage(2),
        6: part_stage, 8: cond_stage, 10: row_stage,
    }

    for_sibling(-1)

    def iteration(step, unused):
        i = step - 1
        for_sibling(i + 1)
        for_owners(i)
        over_z(i)
        settle(i)
        for at, stage in hooks.items():
            pl.when(i == at)(stage)
        return unused

    lax.fori_loop(0, chunks + 1 + Z_LAG, iteration, 0)

    square_in[s] = jnp.zeros((8, 128), f32) + jnp.sum(squares[...])
    begin("square")

    cond_gram = jnp.zeros((images, images), f32)
    for o in range(SHARDS):
        cond_gram += nt(cond_ref[o], cond_ref[o])

    def gram(c, value):
        return value + nt(d_blocks_ref[c], d_blocks_ref[c])

    d_gram = lax.fori_loop(0, 6 * NB, gram, jnp.zeros((images, images), f32))
    got("square")
    value = square_in[0]
    for o in range(1, SHARDS):
        value += square_in[o]
    norm_ref[...] = value + jnp.sum(cond_gram * d_gram)

    def finish(j, unused):
        span = pl.ds(j * ch, ch)
        pltpu.make_async_copy(final.at[span], grads_ref.at[span], keep_sem.at[j]).wait()
        rank = along(j)[0]

        @pl.when(rank == 0)
        def _():
            z_copy("rise", j).wait_send()

        @pl.when(rank >= 2)
        def _():
            z_copy("sink", j).wait_send()

        @pl.when(rank == 1)
        def _():
            z_copy("final_down", j).wait_send()

        @pl.when(jnp.logical_or(rank == 1, rank == 2))
        def _():
            z_copy("final_up", j).wait_send()

        return unused

    lax.fori_loop(0, chunks, finish, 0)
    for name in ("d_far", "stat_far", "tok_far", "tok", "d", "stat", "part", "pre", "square"):
        for copy in small_copies(name):
            copy.wait_send()


def collect(cap, left_of, right_of, row_of, col_of, count, acts, dmod, ends, stats, times, conds, freq_low, label, own_pre, own_cond,
            row_master, tile_master):
    per = tile_master.shape[0]
    ch = next(n for n in (2, 1) if cap % n == 0)
    chunks = cap // ch
    images = GROUPS * SHARDS
    vmem = pl.BlockSpec(memory_space=pltpu.VMEM)
    smem = pl.BlockSpec(memory_space=pltpu.SMEM)
    anywhere = pl.BlockSpec(memory_space=pl.ANY)
    small = 9 + 6 * (SHARDS - 1)
    dma = pltpu.SemaphoreType.DMA

    def blocks(*lead):
        return pltpu.VMEM(lead + (BLK, BLK), bf16)

    return pl.pallas_call(
        functools.partial(collect_body, cap, ch),
        out_shape=[
            jax.ShapeDtypeStruct((per, BLK, BLK), bf16),
            jax.ShapeDtypeStruct((6 * NB, images, BLK), bf16),
            jax.ShapeDtypeStruct(row_master.shape, f32),
            jax.ShapeDtypeStruct((8, 128), f32),
            jax.ShapeDtypeStruct((8, 128), f32),
        ],
        in_specs=[smem] * 5 + [vmem] * 11 + [anywhere],
        out_specs=[anywhere] + [vmem] * 4,
        scratch_shapes=[
            blocks(RING, 4, ch),
            blocks(RING, 4, ch),
            blocks(RING, ch),
            blocks(RING, ch),
            blocks(RING, ch),
            pltpu.VMEM((RING, ch, BLK // 2, BLK), bf16),
            pltpu.VMEM((RING, ch, BLK // 2, BLK), bf16),
            blocks(RING, ch),
            blocks(RING, ch),
            blocks(cap),
            blocks(cap),
            blocks(cap),
            blocks(cap),
            pltpu.VMEM((per // 3, BLK, BLK), f32),
            pltpu.VMEM((per, images, BLK), f32),
            pltpu.VMEM((images * 8 * LANES, 128), bf16),
            pltpu.VMEM((images * 8 * LANES, 128), f32),
            pltpu.VMEM((images * 8, 128), f32),
            pltpu.VMEM((SHARDS, TOKEN_ROWS, 128), f32),
            pltpu.VMEM((GROUPS, TOKEN_ROWS, 128), f32),
            pltpu.VMEM((TOKEN_ROWS, 128), f32),
            pltpu.VMEM((SHARDS, images, 128), f32),
            pltpu.VMEM((SHARDS, images, 128), f32),
            pltpu.VMEM((SHARDS, images, 128), f32),
            pltpu.VMEM((SHARDS, images, 128), f32),
            pltpu.VMEM((images, 128), f32),
            pltpu.VMEM((images, 128), f32),
            pltpu.VMEM((24, 128), f32),
            pltpu.VMEM((8, BLK), f32),
            pltpu.VMEM((SHARDS, 8, 128), f32),
            dma((RING, 4)),
            dma((RING, 4)),
            dma((RING, 2)),
            dma((RING,)),
            dma((RING,)),
            dma((RING,)),
            dma((RING,)),
            dma((RING,)),
            dma((RING,)),
            dma((chunks,)),
            dma((chunks,)),
            dma((chunks,)),
            dma((chunks,)),
            dma((2, chunks)),
            dma((chunks,)),
            dma,
            dma((small,)),
            dma((small,)),
        ],
        compiler_params=pltpu.CompilerParams(
            collective_id=100 + cap, has_side_effects=True, vmem_limit_bytes=61 << 20
        ),
        name="collect",
    )(left_of, right_of, row_of, col_of, count, acts, dmod, ends, stats, times, conds, freq_low, label, own_pre, own_cond,
      row_master, tile_master)


def positions(grid_side, model_width):
    index = jnp.arange(grid_side * grid_side)
    row_pos = (index // grid_side).astype(f32)
    col_pos = (index % grid_side).astype(f32)
    quarter = model_width // 4
    omega = 1.0 / 10000.0 ** (jnp.arange(quarter, dtype=f32) / quarter)
    row_arg = row_pos[:, None] * omega[None, :]
    col_arg = col_pos[:, None] * omega[None, :]
    return jnp.concatenate([jnp.sin(row_arg), jnp.cos(row_arg), jnp.sin(col_arg), jnp.cos(col_arg)], axis=1)


def time_freq(step_values, freq_width):
    half_width = freq_width // 2
    freqs = jnp.exp(-math.log(10000.0) * jnp.arange(half_width, dtype=f32) / half_width)
    angle_arg = step_values.astype(f32)[:, None] * freqs[None, :]
    return jnp.concatenate([jnp.cos(angle_arg), jnp.sin(angle_arg)], axis=1)


def silu_slope(value):
    gate = jax.nn.sigmoid(value)
    return gate * (1.0 + value * (1.0 - gate))


def blocked(array):
    count = array.shape[0]
    return array.reshape(count, -1, BLK).transpose(1, 0, 2)


def factors_of(assign):
    n = jnp.maximum(assign - ADA, 0)
    out, up, down = n - AT_OUT, n - AT_UP, n - AT_DOWN
    left = jnp.where(
        n < AT_OUT,
        L_ATT + n // QB,
        jnp.where(n < AT_UP, L_OUT + out // NB, jnp.where(n < AT_DOWN, L_MLP + up // HB, L_HID + down // NB)),
    )
    right = jnp.where(
        n < AT_OUT,
        R_QKV + n % QB,
        jnp.where(n < AT_UP, R_OUT + out % NB, jnp.where(n < AT_DOWN, R_UP + up % HB, R_DOWN + down % NB)),
    )
    return left.astype(jnp.int32), right.astype(jnp.int32)


def spread_plain(slot_of, row_of, col_of, tile_master, row_master, timesteps, labels):
    shard_count = lax.axis_size("shard")
    everyone = ("grp", "shard")
    me = lax.axis_index("shard")
    per, columns = tile_master.shape[0], row_master.shape[1]
    low_rows = row_master.astype(bf16)
    at = [0]

    def take(count):
        at[0] += count
        return low_rows[at[0] - count : at[0]]

    table, w_time1, w_time2 = take(NCLASS), take(FREQ), take(D)
    w_final = (take(D), take(D))
    take(2 * PATCH_DIM)
    take(1)
    b_time1, b_time2 = take(1), take(1)
    take(4)
    b_ada = take(6)
    take(FF // D)
    b_final = take(2)
    b_mod = jnp.concatenate([b_ada, b_final], axis=0)

    packed = pack_tiles(slot_of, tile_master)
    gathered = lax.all_gather(packed, "shard", axis=0, tiled=True)
    near = lax.all_gather(low_rows[NEAR_START:], "shard", axis=1, tiled=True)
    near = jnp.pad(near, ((0, NEAR - NEAR_REAL), (0, 0))).reshape(NEAR, LANES, 128).transpose(1, 0, 2)

    ids = lax.all_gather(jnp.concatenate([timesteps, labels]), everyone, axis=0)
    all_steps, all_labels = ids[:, 0], ids[:, 1]
    freq_low = time_freq(all_steps, FREQ).astype(bf16)
    own_pre = nn(freq_low, w_time1) + b_time1
    time_low = lax.all_gather(jax.nn.silu(own_pre).astype(bf16), "shard", axis=1, tiled=True)
    one_hot = (all_labels[:, None] == jnp.arange(NCLASS, dtype=jnp.int32)[None, :]).astype(bf16)
    own_cond = nn(time_low, w_time2) + b_time2 + nn(one_hot, table)
    cond_low = lax.all_gather(jax.nn.silu(own_cond).astype(bf16), "shard", axis=1, tiled=True)
    group_cond = lax.dynamic_slice(cond_low, (lax.axis_index("grp") * shard_count, 0), (shard_count, D))
    part_mod = ada_front(row_of, col_of, blocked(group_cond), tile_master)
    part_mod = part_mod.transpose(1, 0, 2).reshape(shard_count, 6, D)
    part_final = jnp.stack([nn(group_cond, w_final[0]), nn(group_cond, w_final[1])], axis=1)
    spread = jnp.zeros((shard_count, 8, D), f32)
    spread = lax.dynamic_update_slice(
        spread,
        jnp.concatenate([jnp.zeros((shard_count, 6, columns), f32), part_final], axis=1) + b_mod[None].astype(f32),
        (0, 0, me * columns),
    )
    spread = spread + jnp.concatenate([part_mod, jnp.zeros((shard_count, 2, D), f32)], axis=1)
    mods = lax.psum_scatter(spread, "shard", scatter_dimension=0, tiled=True)[0]
    label = jnp.broadcast_to(all_labels.astype(f32)[:, None], (all_labels.shape[0], 128))

    def lanes(array):
        return array.reshape(-1, LANES, 128).transpose(1, 0, 2)

    return (
        gathered, near, mods.reshape(8 * LANES, 128), freq_low, label, lanes(time_low), lanes(cond_low), own_pre, own_cond,
    )


def collect_plain(left_of, right_of, row_of, col_of, count, acts, dmod, ends, stats, times, conds, freq_low, label, own_pre, own_cond,
                  row_master, tile_master):
    everyone = ("grp", "shard")
    me = lax.axis_index("shard")
    columns = row_master.shape[1]
    low_rows = row_master.astype(bf16)
    w_time2 = low_rows[NCLASS + FREQ : NCLASS + FREQ + D]
    w_final = [low_rows[NCLASS + FREQ + (1 + i) * D : NCLASS + FREQ + (2 + i) * D] for i in range(2)]
    one_hot = (label[:, :1].astype(jnp.int32) == jnp.arange(NCLASS, dtype=jnp.int32)[None, :]).astype(bf16)
    time_low, cond_low = (array.transpose(1, 0, 2).reshape(-1, D) for array in (times, conds))
    partial = tile_grads(left_of, right_of, acts)
    own_tiles = lax.psum_scatter(partial, "shard", scatter_dimension=0, tiled=True)
    own_tiles = lax.psum(own_tiles, "grp")

    all_dmod = lax.all_gather(dmod.reshape(1, -1).astype(bf16), everyone, axis=0, tiled=True)
    dmod_blocks = blocked(all_dmod[:, : 6 * D])
    own_dmod = lax.dynamic_slice(all_dmod.reshape(-1, 8, D), (0, 0, me * columns), (all_dmod.shape[0], 8, columns))
    part_cond = ada_back(row_of, col_of, dmod_blocks, tile_master).transpose(1, 0, 2).reshape(-1, D)
    part_cond = part_cond + nt(own_dmod[:, 6], w_final[0]) + nt(own_dmod[:, 7], w_final[1])
    own_dcond = lax.psum_scatter(part_cond, "shard", scatter_dimension=1, tiled=True) * silu_slope(own_cond)
    dcond_low = own_dcond.astype(bf16)
    own_dpre = lax.psum_scatter(nt(dcond_low, w_time2), "shard", scatter_dimension=1, tiled=True)
    own_dpre = own_dpre * silu_slope(own_pre)
    wide_dmod = own_dmod.astype(f32)

    token_rows = ends.transpose(1, 0, 2).reshape(TOKEN_ROWS, D)
    token_rows = lax.psum_scatter(token_rows, "shard", scatter_dimension=1, tiled=True)
    token_rows = lax.psum(token_rows, "grp")
    own_rows = jnp.concatenate(
        [
            tn(one_hot.astype(f32), own_dcond),
            tn(freq_low, own_dpre.astype(bf16)),
            tn(time_low, dcond_low),
            tn(cond_low, own_dmod[:, 6]),
            tn(cond_low, own_dmod[:, 7]),
            token_rows[: T_PATCH + 1],
            jnp.sum(own_dpre, axis=0)[None],
            jnp.sum(own_dcond, axis=0)[None],
            token_rows[T_QUERY : T_VALUE + 1],
            token_rows[T_OUT : T_DOWN + 1],
            jnp.sum(wide_dmod[:, :6], axis=0),
            token_rows[T_UP:T_END],
            jnp.sum(wide_dmod[:, 6:], axis=0),
        ],
        axis=0,
    )
    whole_stats = lax.psum(stats[:4, 0], everyone)
    cond_gram = nt(cond_low, cond_low)
    dmod_gram = nt(all_dmod[:, : 6 * D], all_dmod[:, : 6 * D])
    counted = jnp.arange(own_tiles.shape[0], dtype=jnp.int32) < count
    wide_tiles = jnp.where(counted[:, None, None], own_tiles.astype(f32), 0.0)
    square_part = jnp.sum(wide_tiles * wide_tiles) + jnp.sum(own_rows * own_rows)
    square_sum = lax.psum(square_part, "shard") + jnp.sum(cond_gram * dmod_gram)
    return own_tiles, dmod_blocks, own_rows, square_sum, whole_stats


def pack_body(slot_ref, tile_ref, out_ref):
    out_ref[...] = tile_ref[...].astype(bf16)


def pack_tiles(slot_of, tile_master):
    per = tile_master.shape[0]
    return pl.pallas_call(
        pack_body,
        grid_spec=pltpu.PrefetchScalarGridSpec(
            num_scalar_prefetch=1,
            grid=(per,),
            in_specs=[pl.BlockSpec((1, BLK, BLK), lambda p, slots: (slots[p], 0, 0))],
            out_specs=pl.BlockSpec((1, BLK, BLK), lambda p, slots: (p, 0, 0)),
        ),
        out_shape=jax.ShapeDtypeStruct(tile_master.shape, bf16),
        name="pack_tiles",
    )(slot_of, tile_master)


def shards(
    patches, noise, timesteps, labels, assign, tile_master, tile_bases, tile_moment, tile_second,
    row_master, row_moment, row_second,
):
    group_count, shard_count = lax.axis_size("grp"), lax.axis_size("shard")
    everyone = ("grp", "shard")
    me = lax.axis_index("shard")
    per = tile_master.shape[0]
    columns = row_master.shape[1]
    token_total = patches.shape[0] * group_count * shard_count
    tile_total = assign.shape[0]

    slot_ids = jnp.arange(tile_total, dtype=jnp.int32)
    mine = lax.dynamic_slice(assign, (me * per,), (per,))
    row_of = jnp.where(mine < ADA, mine // (6 * NB), 0).astype(jnp.int32)
    col_of = jnp.where(mine < ADA, mine % (6 * NB), -1).astype(jnp.int32)
    owned = assign.reshape(-1, per)
    local = jnp.arange(per, dtype=jnp.int32)
    ahead = (owned[:, None, :] % tile_total < ADA).astype(jnp.int32) * per + local[None, None, :]
    behind = (owned[:, :, None] < ADA).astype(jnp.int32) * per + local[None, :, None]
    rank = jnp.sum((ahead < behind).astype(jnp.int32), axis=2)
    place = (rank + jnp.arange(owned.shape[0], dtype=jnp.int32)[:, None] * per).reshape(-1)
    ordered = jnp.sum(jnp.where(place[None, :] == slot_ids[:, None], assign[None, :], 0), axis=1)
    inverse = jnp.sum(jnp.where(assign[None, :] == slot_ids[:, None], place[None, :], 0), axis=1)
    rank = lax.dynamic_slice(rank, (me, 0), (1, per))[0]
    slot_of = jnp.sum(jnp.where(rank[None, :] == local[:, None], local[None, :], 0), axis=1)

    fast = group_count == GROUPS and shard_count == SHARDS
    if fast:
        freq = time_freq(timesteps, FREQ).reshape(2, 128)
        ids = jnp.concatenate([freq, jnp.broadcast_to(labels.astype(f32)[:, None], (1, 128)), jnp.zeros((5, 128), f32)], axis=0)
        gathered, near, mods, freq_low, label, times, conds, own_pre, own_cond = spread(
            per, slot_of, row_of, col_of, tile_master, row_master, ids
        )
        gathered = gathered.reshape(tile_total, BLK, BLK)
    else:
        gathered, near, mods, freq_low, label, times, conds, own_pre, own_cond = spread_plain(
            slot_of, row_of, col_of, tile_master, row_master, timesteps, labels
        )

    loss_scale = 1.0 / (token_total * PATCH_DIM)
    acts, dmod, ends, stats = block_step(
        inverse[ADA:], gathered, patches, noise, positions(LAT // PATCH_SIDE, D), near, mods.reshape(8 * LANES, 128),
        2.0 * loss_scale,
    )

    left_of, right_of = factors_of(ordered)
    count = jnp.sum((col_of < 0).astype(jnp.int32)).reshape(1)
    if fast:
        own_tiles, dmod_blocks, own_rows, squares, totals = collect(
            per, left_of, right_of, row_of, col_of, count, acts, dmod, ends, stats, times, conds, freq_low, label, own_pre,
            own_cond, row_master, tile_master,
        )
        square_sum, whole_stats = squares[0, 0], totals[:4, 0]
    else:
        own_tiles, dmod_blocks, own_rows, square_sum, whole_stats = collect_plain(
            left_of, right_of, row_of, col_of, count, acts, dmod, ends, stats, times, conds, freq_low, label, own_pre,
            own_cond, row_master, tile_master,
        )
    grad_norm = jnp.sqrt(square_sum)
    factor = clip_at / jnp.maximum(grad_norm, clip_at)

    images = conds.shape[1]
    cond_columns = conds.reshape(NB, 2, images, 128).transpose(0, 1, 3, 2).reshape(NB, BLK, images)
    new_tile_moment, new_tile_second, tile_update = adam(
        rank, row_of, col_of, factor.reshape(1), own_tiles, cond_columns, dmod_blocks,
        tile_bases, tile_moment, tile_second,
    )
    row_grad = factor * own_rows
    new_row_moment = beta_one * row_moment + (1.0 - beta_one) * row_grad
    new_row_second = beta_two * row_second + (1.0 - beta_two) * row_grad * row_grad
    row_update = -rate_step * (new_row_moment / (jnp.sqrt(new_row_second) + adam_eps) + decay_rate * row_master)
    loss = whole_stats[0] / (token_total * PATCH_DIM)
    act_rms = jnp.sqrt(whole_stats[1:] / (token_total * D))
    return (
        loss, grad_norm, act_rms, new_tile_moment, new_tile_second, tile_update, new_row_moment, new_row_second, row_update,
    )


def solution(mesh):
    placed = (
        P(("grp", "shard"), None),
        P(("grp", "shard"), None),
        P(("grp", "shard")),
        P(("grp", "shard")),
        P(),
        P("shard", None, None),
        P("shard", None, None, None),
        P("shard", None, None),
        P("shard", None, None),
        P(None, "shard"),
        P(None, "shard"),
        P(None, "shard"),
    )
    return jax.shard_map(
        shards,
        mesh=mesh,
        in_specs=placed,
        out_specs=(
            P(), P(), P(),
            P("shard", None, None), P("shard", None, None), P("shard", None, None),
            P(None, "shard"), P(None, "shard"), P(None, "shard"),
        ),
        check_vma=False,
    )
```

time: 1290 us -> 486 us (0.38); the launches traced: 1280 us -> 485 us
  waiting for transfers between devices: 582 us -> 0 us
  Pallas kernels: 0 us -> 449 us
  local copies, waits for them, and re-layouts: 379 us -> 15.6 us
  matrix products: 185 us -> 0 us
  blocking collectives: 58.1 us -> 0 us
  other arithmetic: 50.4 us -> 14.5 us
  between operations: 21 us -> 5.76 us
    pallas_call x0 -> x4, Pallas kernels: none -> 449 us  [the longest x1 208 us: collect(): pl.pallas_call(functools.partial(collect_body, cap, ch), out_shape=[jax.S...]
    reduce_scatter x1 -> x0, waiting for transfers between devices: 223 us -> none  [shards(): lax.psum_scatter(grad_slots.astype(jnp.bfloat16), 'shard', scatter_dimens...]
    all_gather x2 -> x0, waiting for transfers between devices: 212 us -> none  [the longest x1 164 us: shards(): lax.all_gather(tile_master.astype(jnp.bfloat16), 'shard', axis=0, tiled=T...]
    dot_general x35 -> x0, matrix products: 185 us -> none  [the longest x1 28.8 us: shards(): jnp.einsum('sji,sjk->sik', left_basis, jnp.einsum('sij,sjk->sik', tile_gr...]
    psum x1 -> x0, waiting for transfers between devices: 147 us -> none  [shards(): lax.psum(own_tiles.astype(jnp.bfloat16), 'grp').astype(jnp.float32)]
    unnamed x162 -> x40, local copies, waits for them, and re-layouts: 129 us -> 11.7 us
    reshape x9 -> x1, local copies, waits for them, and re-layouts: 73.3 us -> 0.86 us  [shards(): conds.reshape(NB, 2, images, 128).transpose(0, 1, 3, 2)]
    psum x2 -> x0, blocking collectives: 58.1 us -> none  [the longest x1 43.5 us: shards(): whole_stats = lax.psum(statistics, ('grp', 'shard'))]
  transfers between devices with their start and end apart: 5 -> 0, of which waited for: 4 -> 0; matrix products, arithmetic and copies ran while one was open for 14% -> 0% of each run, Pallas kernels for 0% -> 0%
where the time goes in v1:
time: 486 us; the launch traced here: 485 us
  Pallas kernels  449 us (92%)
  local copies, waits for them, and re-layouts  15.6 us (3%)
  other arithmetic  14.5 us (3%)
  between operations  5.76 us (1%)
    pallas_call x1, Pallas kernels, collect(): pl.pallas_call(functools.partial(collect_body, cap, ch), out_shape=[jax.S...  208 us
    pallas_call x1, Pallas kernels, spread(): pl.pallas_call(functools.partial(spread_body, cap, n_third), out_shape=[j...  136 us
    pallas_call x1, Pallas kernels, block_step(): pl.pallas_call(functools.partial(block_body, loss_factor), out_shape=[jax...  68.8 us
    pallas_call x1, Pallas kernels, adam(): pl.pallas_call(functools.partial(adam_body, group), grid_spec=pltpu.Prefe...  36.6 us
    unnamed x40, local copies, waits for them, and re-layouts  11.7 us

profile of v1, /device:TPU:0, one launch (start us, length us, event | category | flops | bytes accessed | tf_op | source)
XLA Modules:
  0.0 484.5 jit_solution(12326709887058060409)
XLA Ops:
  0.6 1.4 fusion.26
  2.1 0.0 copy-start.10
  2.1 0.0 copy-start.11
  2.1 0.7 broadcast_remainder_fusion
  2.7 0.1 mul.124
  2.8 0.1 copy.35
  2.9 0.1 rem.121
  3.0 0.8 convert_reduce_fusion
  3.8 0.2 dynamic-slice_reduce_fusion.where_ref
  4.0 0.0 copy-start.17
  4.0 0.1 select_reduce_fusion.2.slot_ref
  4.7 0.1 fusion.27
  5.5 0.1 pad.5.clone
  5.5 0.1 pad.6.clone
  5.6 0.1 maximum_maximum_fusion.ids_ref
  5.7 0.0 copy-start
  5.7 3.7 copy-done
  9.4 0.0 copy-start.1
  9.4 1.6 copy-done.1
  11.0 135.6 %spread.1 = (bf16[8,36,256,256]{3,2,1,0:T(8,128)(2,1)}, bf16[8,64,128]{2,1,0:T(8,128)(2,1)S(1)}, f32[64,128]{1,0:T(8,128)S(1)}, bf16[32,256]{1,0:T(8,128)(2,1)S(...) custom-call(s32[36]{0:T(128)S(1)} %select_reduce_fusion.2.slot_ref, ...), custom_call_target="tpu_custom_call" | custom-call | tf_op jit(solution)/shard_map/spread/pallas_call | solution.py:860
  146.6 0.0 copy-done.10
  146.6 0.0 copy-done.11
  146.6 0.0 copy-done.17
  146.6 0.0 copy-start.3
  146.6 0.6 copy-done.3
  147.2 0.0 copy-start.5
  147.2 0.6 copy-done.5
  147.9 0.0 copy-start.6
  147.9 0.6 copy-done.6
  148.5 0.0 copy-start.7
  148.5 0.6 copy-done.7
  149.1 0.0 copy-start.8
  149.1 0.6 copy-done.8
  149.7 0.0 copy-start.9
  149.7 0.6 copy-done.9
  150.3 0.0 copy-start.12
  150.3 0.7 copy-done.12
  150.9 0.0 copy-start.13
  150.9 0.6 copy-done.13
  151.6 1.9 multiply_sine_fusion.1
  153.5 1.1 pad_maximum_fusion.spot_ref
  154.6 0.1 copy.36
  154.6 0.1 broadcast_add_fusion
  154.7 0.1 add.168
  154.8 0.0 copy-done.15
  154.8 0.2 select_reduce_fusion
  155.0 0.6 slice.17.place_ref
  155.6 0.0 copy-done.14
  155.6 0.8 copy.38.noise_ref
  156.4 0.0 copy-done.16
  156.4 0.7 copy.37.patches_ref
  157.1 68.8 %block_step.1 = (bf16[64,256,256]{2,1,0:T(8,128)(2,1)}, f32[64,128]{1,0:T(8,128)}, f32[8,48,128]{2,1,0:T(8,128)}, f32[8,128]{1,0:T(8,128)}) custom-call(s32[192]{0:T(256)} %slice.17.place_ref, bf16[288,256,256]{2,1,0:T(8,128)(2,1)} %bitcast.15, bf16[256,16]{1,0:T(8,128)(2,1)} %copy.37.patches_ref, f32[256,16]{1,0:T(8,128)} %copy.38.noise_ref, ...), custom_call_target="tpu_custom_call" | custom-call | flops 19327352832 | bytes 50331648 | tf_op jit(solution)/shard_map/block_step/pallas_call | solution.py:417
  225.9 0.6 fusion.9
  226.5 207.6 %collect.1 = (bf16[36,256,256]{2,1,0:T(8,128)(2,1)}, bf16[24,32,256]{2,1,0:T(8,128)(2,1)}, f32[4379,128]{1,0:T(8,128)}, f32[8,128]{1,0:T(8,128)}, f32[8,128]{1,0:T(8,128)}) custom-call(s32[288]{0:T(512)} %get-tuple-element.64.left_ref, s32[288]{0:T(512)} %get-tuple-element.63.right_ref, s32[36]{0:T(128)} %copy-done.11, s32[36]{0:T(128)} %copy-done.10, ...), custom_call_target="tpu_custom_call" | custom-call | tf_op jit(solution)/shard_map/collect/pallas_call | solution.py:1429
  434.2 1.2 slice.19
  436.1 0.0 copy-done.2
  436.1 0.0 copy-start.4
  436.1 6.9 %add_multiply_fusion = (f32[4379,128]{1,0:T(8,128)}, f32[4379,128]{1,0:T(8,128)}, f32[4379,128]{1,0:T(8,128)}) fusion(f32[4379,128]{1,0:T(8,128)S(1)} %copy-done.2, f32[4379,128]{1,0:T(8,128)} %get-tuple-element.50, f32[]{:T(128)} %div.103, f32[4379,128]{1,0:T(8,128)} %param.23, f32[4379,128]{1,0:T(8,128)} %param.22), kind=kLoop, calls=%fused_computation.3 | loop fusion | flops 6726144 | bytes 15694340 | tf_op jit(solution)/shard_map/mul | solution.py:1746
  443.0 0.0 copy-done.4
  443.0 0.9 copy.39
  443.9 36.6 %adam_tiles.1 = (f32[36,256,256]{2,1,0:T(8,128)}, f32[36,256,256]{2,1,0:T(8,128)}, f32[36,256,256]{2,1,0:T(8,128)}) custom-call(s32[36]{0:T(128)} %copy-done.17, s32[36]{0:T(128)} %copy-done.11, s32[36]{0:T(128)} %copy-done.10, f32[1]{0:T(128)} %bitcast.7.factor_ref, bf16[36,256,256]{2,1,0:T(8,128)(2,1)} %get-tuple-element.45.grads_ref, ...), custom_call_target="tpu_custom_call" | custom-call | tf_op jit(solution)/shard_map/adam_tiles/pallas_call | solution.py:571
  480.5 0.0 copy-done.18
  480.5 0.5 slice.18
  481.6 0.6 sqrt_reduce_fusion
  (12 shorter events, 0.1 us)
Async XLA Ops:
  2.1 144.5 %copy-start.10 = (s32[36]{0:T(128)}, s32[36]{0:T(128)S(1)}, u32[]{:S(2)}) copy-start(s32[36]{0:T(128)S(1)} %get-tuple-element.57.col_ref) | copy-start | bytes 436
  2.1 144.5 %copy-start.11 = (s32[36]{0:T(128)}, s32[36]{0:T(128)S(1)}, u32[]{:S(2)}) copy-start(s32[36]{0:T(128)S(1)} %get-tuple-element.62.row_ref) | copy-start | bytes 436
  4.0 142.6 %copy-start.17 = (s32[36]{0:T(128)}, s32[36]{0:T(128)S(1)}, u32[]{:S(2)}) copy-start(s32[36]{0:T(128)S(1)} %dynamic-slice_reduce_fusion.where_ref) | copy-start | bytes 436
  5.7 3.7 copy-start
  9.4 1.6 copy-start.1
  146.6 0.6 copy-start.3
  147.2 0.6 copy-start.5
  147.9 0.6 copy-start.6
  148.5 0.6 copy-start.7
  149.1 0.6 copy-start.8
  149.7 0.6 copy-start.9
  150.3 0.7 copy-start.12
  150.9 0.6 copy-start.13
  151.5 3.3 copy-start.15
  151.5 4.1 copy-start.14
  151.5 4.8 copy-start.16
  226.5 209.6 %copy-start.2 = (f32[4379,128]{1,0:T(8,128)S(1)}, f32[4379,128]{1,0:T(8,128)}, u32[]{:S(2)}) copy-start(f32[4379,128]{1,0:T(8,128)} %rows_ref.3) | copy-start | bytes 6726148
  436.1 6.9 %copy-start.4 = (bf16[8,32,128]{2,1,0:T(8,128)(2,1)S(1)}, bf16[8,32,128]{2,1,0:T(8,128)(2,1)}, u32[]{:S(2)}) copy-start(bf16[8,32,128]{2,1,0:T(8,128)(2,1)} %copy-done.3) | copy-start | bytes 196612
  443.9 36.6 %copy-start.18 = (f32[8,128]{1,0:T(8,128)S(1)}, f32[8,128]{1,0:T(8,128)}, u32[]{:S(2)}) copy-start(f32[8,128]{1,0:T(8,128)} %get-tuple-element.43) | copy-start | bytes 12292

commit v2 on v1

--- a/solution.py
+++ b/solution.py
@@ -34,6 +34,7 @@
 ACTS = R_DOWN + NB
 B_OUT, B_UP, B_DOWN = QB, QB + NB, QB + NB + HB
 ROW_STEP = 16
+ADAM_GROUP = 3
 LANES = D // 128
 NEAR = 64
 NEAR_START = NCLASS + FREQ + 3 * D
@@ -45,6 +46,7 @@
 T_END = T_UP + FF // D
 TOKEN_ROWS = 48
 
+CAPS = (28, 30)
 GROUPS, SHARDS = 4, 8
 MESH_ID = pl.DeviceIdType.MESH
 
@@ -183,9 +185,14 @@
         sums[which] = sums[which] + fold(value)
 
     patches = patches_ref[...]
+    side = LAT // PATCH_SIDE
     for r in range(NB):
-        span = slice(r * BLK, (r + 1) * BLK)
-        stream[r] = nn(patches, near_block(0, r)) + row_block(N_PATCH, r) + spot_ref[:, span]
+        stream[r] = tn(patches, near_block(0, r)) + row_block(N_PATCH, r)
+    for i in range(side):
+        span = slice(i * side, (i + 1) * side)
+        for r in range(2):
+            stream[r, span, :] = stream[r, span, :] + spot_ref[r, i : i + 1, :]
+            stream[2 + r, span, :] = stream[2 + r, span, :] + spot_ref[r]
 
     def modulate(source, scale, shift):
         def body(at):
@@ -278,9 +285,9 @@
         put(low_in, 0, at, norm * (1.0 + mod(7)) + mod(6))
 
     over_rows(end_step)
-    predicted = nt(low_in[0], near_block(PATCH_DIM, 0))
+    predicted = nt(near_block(PATCH_DIM, 0), low_in[0])
     for r in range(1, NB):
-        predicted += nt(low_in[r], near_block(PATCH_DIM, r))
+        predicted += nt(near_block(PATCH_DIM, r), low_in[r])
     mismatch = predicted - noise_ref[...]
     loss_sum = jnp.sum(mismatch * mismatch)
     pred_low = (loss_factor * mismatch).astype(bf16)
@@ -289,8 +296,8 @@
             ends_ref[2 * r + i, row : row + count, :] = value[:, i * 128 : (i + 1) * 128]
 
     for r in range(NB):
-        put_rows(PATCH_DIM, PATCH_DIM, r, tn(pred_low, low_in[r]))
-        flow[r] = nn(pred_low, near_block(PATCH_DIM, r))
+        put_rows(PATCH_DIM, PATCH_DIM, r, nn(pred_low, low_in[r]))
+        flow[r] = tn(pred_low, near_block(PATCH_DIM, r))
 
     def end_back(at):
         grad = wide(flow, at)
@@ -385,7 +392,7 @@
 
     over_rows(first_back)
     for r in range(NB):
-        put_rows(0, PATCH_DIM, r, tn(patches, low_in[r]))
+        put_rows(0, PATCH_DIM, r, nn(patches, low_in[r]))
 
     def total_of(which):
         return jnp.sum(sums[which], axis=0, keepdims=True)
@@ -534,60 +541,76 @@
     )(left_of, right_of, acts)
 
 
-def adam_body(group, where_ref, row_ref, col_ref, factor_ref, grads_ref, cond_ref, dmod_ref, bases_ref, moment_ref, second_ref,
-              new_moment_ref, new_second_ref, update_ref, grad):
+def adam_body(
+    group, where_ref, row_ref, col_ref,
+    norm_ref, grads_ref, cond_ref, dmod_ref, bases_ref, moment_ref, second_ref, row_grad_ref, row_master_ref, row_moment_ref, row_second_ref,
+    new_moment_ref, new_second_ref, update_ref, new_row_moment_ref, new_row_second_ref, row_update_ref,
+):
     step = pl.program_id(0)
-    factor = factor_ref[0]
+    factor = clip_at / jnp.maximum(jnp.sqrt(norm_ref[0:1, 0:1]), clip_at)
+
+    def moved(moment, second, grad):
+        new_moment = beta_one * moment + (1.0 - beta_one) * grad
+        new_second = beta_two * second + (1.0 - beta_two) * grad * grad
+        return new_moment, new_second, new_moment / (jnp.sqrt(new_second) + adam_eps)
+
     for j in range(group):
         s = step * group + j
-
-        @pl.when(col_ref[s] >= 0)
-        def _():
-            grad[...] = nn(cond_ref[row_ref[s]], dmod_ref[jnp.maximum(col_ref[s], 0)]).astype(bf16)
-
-        @pl.when(col_ref[s] < 0)
-        def _():
-            grad[...] = grads_ref[where_ref[s]]
-
+        r, c = row_ref[s], col_ref[s]
+        cond = jnp.concatenate([cond_ref[2 * r], cond_ref[2 * r + 1]], axis=1)
+        thin = tn(cond, dmod_ref[jnp.maximum(c, 0)]).astype(bf16)
+        grad = jnp.where(c >= 0, thin, grads_ref[where_ref[s]])
         left, right = bases_ref[j, 0].astype(bf16), bases_ref[j, 1].astype(bf16)
-        turned = factor * nn(left.T, nn(grad[...], right).astype(bf16))
-        moment = beta_one * moment_ref[j] + (1.0 - beta_one) * turned
-        second = beta_two * second_ref[j] + (1.0 - beta_two) * turned * turned
+        turned = factor * tn(left, nn(grad, right).astype(bf16))
+        moment, second, direction = moved(moment_ref[j], second_ref[j], turned)
         new_moment_ref[j] = moment
         new_second_ref[j] = second
-        direction = (moment / (jnp.sqrt(second) + adam_eps)).astype(bf16)
-        update_ref[j] = -rate_step * nt(nn(left, direction).astype(bf16), right)
-
-
-def adam(where, row_of, col_of, factor, grads, cond_blocks, dmod_blocks, bases, moment, second):
+        update_ref[j] = -rate_step * nt(nn(left, direction.astype(bf16)).astype(bf16), right)
+
+    moment, second, direction = moved(row_moment_ref[...], row_second_ref[...], factor * row_grad_ref[...])
+    new_row_moment_ref[...] = moment
+    new_row_second_ref[...] = second
+    row_update_ref[...] = -rate_step * (direction + decay_rate * row_master_ref[...])
+
+
+def adam(where, row_of, col_of, norm, grads, conds, dmod_blocks, bases, moment, second, row_grad, row_master, row_moment, row_second):
     per = moment.shape[0]
-    group = next(g for g in (3, 2, 1) if per % g == 0)
+    group = next(g for g in (ADAM_GROUP, 3, 2, 1) if per % g == 0)
+    steps = per // group
     tile = pl.BlockSpec((group, BLK, BLK), lambda s, *_: (s, 0, 0))
+    row_count, columns = row_master.shape
+    row = pl.BlockSpec((-(-row_count // (8 * steps)) * 8, columns), lambda s, *_: (s, 0))
 
     def whole(array):
         return pl.BlockSpec(array.shape, lambda s, *_: (0,) * array.ndim)
 
     shape = jax.ShapeDtypeStruct(moment.shape, f32)
+    row_shape = jax.ShapeDtypeStruct(row_master.shape, f32)
     return pl.pallas_call(
         functools.partial(adam_body, group),
         grid_spec=pltpu.PrefetchScalarGridSpec(
-            num_scalar_prefetch=4,
-            grid=(per // group,),
+            num_scalar_prefetch=3,
+            grid=(steps,),
             in_specs=[
+                whole(norm),
                 whole(grads),
-                whole(cond_blocks),
+                whole(conds),
                 whole(dmod_blocks),
                 pl.BlockSpec((group, 2, BLK, BLK), lambda s, *_: (s, 0, 0, 0)),
                 tile,
                 tile,
+                row,
+                row,
+                row,
+                row,
             ],
-            out_specs=[tile] * 3,
-            scratch_shapes=[pltpu.VMEM((BLK, BLK), bf16)],
+            out_specs=[tile] * 3 + [row] * 3,
         ),
-        out_shape=[shape] * 3,
-        compiler_params=pltpu.CompilerParams(vmem_limit_bytes=56 << 20),
-        name="adam_tiles",
-    )(where, row_of, col_of, factor, grads, cond_blocks, dmod_blocks, bases, moment, second)
+        out_shape=[shape] * 3 + [row_shape] * 3,
+        compiler_params=pltpu.CompilerParams(vmem_limit_bytes=61 << 20),
+        name="adam",
+    )(where, row_of, col_of, norm, grads, conds, dmod_blocks, bases, moment, second, row_grad, row_master, row_moment, row_second)
+
 
 def spread_body(
     cap, n_third,
@@ -600,7 +623,7 @@
     per = tile.shape[0]
     images = GROUPS * SHARDS
     third = cap // 3
-    step = third // n_third
+    both = cap - 2 * third
     x_at, y_at, c_at, z_at = (z, s ^ 2), (z, s ^ 4), (z, s ^ 1), (z ^ 1, s)
     far_z = [(lax.rem(z + i, GROUPS), s) for i in range(1, GROUPS)]
     near_s = [(z, s ^ i) for i in range(1, SHARDS)]
@@ -646,11 +669,16 @@
     near_copies = to_group(0, lambda p: (near.at[s], near.at[s]))
 
     parity = lax.rem(z, 2)
-    starts = (third + parity * third, 0, 2 * third - parity * third)
+    starts = (both + parity * third, 0, both + third - parity * third)
+
+    def chunk_of(index):
+        kind, at = divmod(index, n_third)
+        size = both if kind == 1 else third
+        first, last = at * size // n_third, (at + 1) * size // n_third
+        return starts[kind] + first, last - first
 
     def chunk(index):
-        kind, at = divmod(index, n_third)
-        return pl.ds(starts[kind] + at * step, step)
+        return pl.ds(*chunk_of(index))
 
     load.wait()
     big = []
@@ -672,14 +700,14 @@
         ).wait_recv()
 
     def pack_chunk(index):
-        kind, at = divmod(index, n_third)
+        start, count = chunk_of(index)
 
         def one(i, unused):
-            p = starts[kind] + at * step + i
+            p = start + i
             pack[p] = tile[slot_ref[p]].astype(bf16)
             return unused
 
-        lax.fori_loop(0, step, one, 0)
+        lax.fori_loop(0, count, one, 0)
 
     def send_mine(index):
         src = pack.at[chunk(index)]
@@ -797,14 +825,16 @@
 
     cut = per // 3
     hooks = [
-        time_stage, cond_stage, group_stage, lambda: ada_stage(0, cut), lambda: ada_stage(cut, cut),
-        lambda: ada_stage(2 * cut, per - 2 * cut), part_stage, mod_stage,
+        (0.10, time_stage), (0.30, cond_stage), (0.50, group_stage), (0.55, lambda: ada_stage(0, cut)),
+        (0.60, lambda: ada_stage(cut, cut)), (0.65, lambda: ada_stage(2 * cut, per - 2 * cut)), (0.70, part_stage), (2.0, mod_stage),
     ]
     seen = [0]
-
-    def hook():
-        if hooks:
-            hooks.pop(0)()
+    steps = [0]
+
+    def hook(last=False):
+        steps[0] += 1
+        while hooks and (last or steps[0] >= hooks[0][0] * 3 * n_third):
+            hooks.pop(0)[1]()
 
     def z_next():
         order = [(w, 2 * n_third + j) for j in range(n_third) for w in (0, 1)]
@@ -836,10 +866,9 @@
         if j % 2:
             z_next()
             hook()
-    while hooks:
-        hook()
     while seen[0] < 3 * n_third:
         z_next()
+    hook(last=True)
     for index in range(3 * n_third):
         wait_for(3, index, s ^ 1)
         for which in range(3):
@@ -851,7 +880,7 @@
 
 def spread(cap, slot_of, row_of, col_of, tile_master, row_master, ids):
     per = tile_master.shape[0]
-    n_third = 4 if cap // 3 % 4 == 0 else next(n for n in (5, 3, 2, 1) if cap // 3 % n == 0)
+    n_third = 5
     images = GROUPS * SHARDS
     vmem = pl.BlockSpec(memory_space=pltpu.VMEM)
     smem = pl.BlockSpec(memory_space=pltpu.SMEM)
@@ -892,7 +921,7 @@
             pltpu.SemaphoreType.DMA((small,)),
             pltpu.SemaphoreType.DMA((small,)),
         ],
-        compiler_params=pltpu.CompilerParams(collective_id=cap, has_side_effects=True, vmem_limit_bytes=40 << 20),
+        compiler_params=pltpu.CompilerParams(collective_id=cap, has_side_effects=True, vmem_limit_bytes=61 << 20),
         name="spread",
     )(slot_of, row_of, col_of, tile_master, row_master, ids)
 
@@ -1347,8 +1376,8 @@
             y_copy(slot2).wait_send()
 
     hooks = {
-        0: spread_stage, 2: order_stage, 3: lambda: ada_stage(0), 4: lambda: ada_stage(1), 5: lambda: ada_stage(2),
-        6: part_stage, 8: cond_stage, 10: row_stage,
+        0: spread_stage, 3: order_stage, 4: lambda: ada_stage(0), 5: lambda: ada_stage(1), 6: lambda: ada_stage(2),
+        7: part_stage, 10: cond_stage, 13: row_stage,
     }
 
     for_sibling(-1)
@@ -1495,15 +1524,11 @@
       row_master, tile_master)
 
 
-def positions(grid_side, model_width):
-    index = jnp.arange(grid_side * grid_side)
-    row_pos = (index // grid_side).astype(f32)
-    col_pos = (index % grid_side).astype(f32)
+def position_table(grid_side, model_width):
     quarter = model_width // 4
     omega = 1.0 / 10000.0 ** (jnp.arange(quarter, dtype=f32) / quarter)
-    row_arg = row_pos[:, None] * omega[None, :]
-    col_arg = col_pos[:, None] * omega[None, :]
-    return jnp.concatenate([jnp.sin(row_arg), jnp.cos(row_arg), jnp.sin(col_arg), jnp.cos(col_arg)], axis=1)
+    angle = jnp.arange(grid_side).astype(f32)[:, None] * omega[None, :]
+    return jnp.stack([jnp.sin(angle), jnp.cos(angle)])
 
 
 def time_freq(step_values, freq_width):
@@ -1650,7 +1675,7 @@
     wide_tiles = jnp.where(counted[:, None, None], own_tiles.astype(f32), 0.0)
     square_part = jnp.sum(wide_tiles * wide_tiles) + jnp.sum(own_rows * own_rows)
     square_sum = lax.psum(square_part, "shard") + jnp.sum(cond_gram * dmod_gram)
-    return own_tiles, dmod_blocks, own_rows, square_sum, whole_stats
+    return own_tiles, dmod_blocks, own_rows, jnp.broadcast_to(square_sum, (8, 128)), whole_stats
 
 
 def pack_body(slot_ref, tile_ref, out_ref):
@@ -1703,8 +1728,10 @@
     if fast:
         freq = time_freq(timesteps, FREQ).reshape(2, 128)
         ids = jnp.concatenate([freq, jnp.broadcast_to(labels.astype(f32)[:, None], (1, 128)), jnp.zeros((5, 128), f32)], axis=0)
-        gathered, near, mods, freq_low, label, times, conds, own_pre, own_cond = spread(
-            per, slot_of, row_of, col_of, tile_master, row_master, ids
+        most = jnp.max(jnp.sum((owned >= ADA).astype(jnp.int32), axis=1))
+        tier = sum((most > cap).astype(jnp.int32) for cap in CAPS)
+        gathered, near, mods, freq_low, label, times, conds, own_pre, own_cond = lax.switch(
+            tier, [functools.partial(spread, cap) for cap in CAPS + (per,)], slot_of, row_of, col_of, tile_master, row_master, ids
         )
         gathered = gathered.reshape(tile_total, BLK, BLK)
     else:
@@ -1714,36 +1741,28 @@
 
     loss_scale = 1.0 / (token_total * PATCH_DIM)
     acts, dmod, ends, stats = block_step(
-        inverse[ADA:], gathered, patches, noise, positions(LAT // PATCH_SIDE, D), near, mods.reshape(8 * LANES, 128),
+        inverse[ADA:], gathered, patches.T, noise.T, position_table(LAT // PATCH_SIDE, D), near, mods.reshape(8 * LANES, 128),
         2.0 * loss_scale,
     )
 
     left_of, right_of = factors_of(ordered)
     count = jnp.sum((col_of < 0).astype(jnp.int32)).reshape(1)
     if fast:
-        own_tiles, dmod_blocks, own_rows, squares, totals = collect(
-            per, left_of, right_of, row_of, col_of, count, acts, dmod, ends, stats, times, conds, freq_low, label, own_pre,
+        own_tiles, dmod_blocks, own_rows, squares, totals = lax.switch(
+            tier, [functools.partial(collect, cap) for cap in CAPS + (per,)], left_of, right_of, row_of, col_of, count, acts, dmod, ends, stats, times, conds, freq_low, label, own_pre,
             own_cond, row_master, tile_master,
         )
-        square_sum, whole_stats = squares[0, 0], totals[:4, 0]
+        whole_stats = totals[:4, 0]
     else:
-        own_tiles, dmod_blocks, own_rows, square_sum, whole_stats = collect_plain(
+        own_tiles, dmod_blocks, own_rows, squares, whole_stats = collect_plain(
             left_of, right_of, row_of, col_of, count, acts, dmod, ends, stats, times, conds, freq_low, label, own_pre,
             own_cond, row_master, tile_master,
         )
-    grad_norm = jnp.sqrt(square_sum)
-    factor = clip_at / jnp.maximum(grad_norm, clip_at)
-
-    images = conds.shape[1]
-    cond_columns = conds.reshape(NB, 2, images, 128).transpose(0, 1, 3, 2).reshape(NB, BLK, images)
-    new_tile_moment, new_tile_second, tile_update = adam(
-        rank, row_of, col_of, factor.reshape(1), own_tiles, cond_columns, dmod_blocks,
-        tile_bases, tile_moment, tile_second,
+    grad_norm = jnp.sqrt(squares[0, 0])
+    new_tile_moment, new_tile_second, tile_update, new_row_moment, new_row_second, row_update = adam(
+        rank, row_of, col_of, squares, own_tiles, conds, dmod_blocks, tile_bases, tile_moment, tile_second,
+        own_rows, row_master, row_moment, row_second,
     )
-    row_grad = factor * own_rows
-    new_row_moment = beta_one * row_moment + (1.0 - beta_one) * row_grad
-    new_row_second = beta_two * row_second + (1.0 - beta_two) * row_grad * row_grad
-    row_update = -rate_step * (new_row_moment / (jnp.sqrt(new_row_second) + adam_eps) + decay_rate * row_master)
     loss = whole_stats[0] / (token_total * PATCH_DIM)
     act_rms = jnp.sqrt(whole_stats[1:] / (token_total * D))
     return (

time: 486 us -> 402 us (0.83)
  Pallas kernels: 449 us -> 381 us
  local copies, waits for them, and re-layouts: 15.6 us -> 3.04 us
    pallas_call x1, Pallas kernels: 208 us -> 173 us  [collect(): pl.pallas_call(functools.partial(collect_body, cap, ch), out_shape=[jax.S...]
    pallas_call x1, Pallas kernels: 136 us -> 104 us  [spread(): pl.pallas_call(functools.partial(spread_body, cap, n_third), out_shape=[j...]
    unnamed x40 -> x4, local copies, waits for them, and re-layouts: 11.7 us -> 0.01 us
    mul x1 -> x0, other arithmetic: 6.91 us -> none  [shards(): -rate_step]
where the time goes in v2:
time: 402 us; the launch traced here: 401 us
  Pallas kernels  381 us (95%)
  other arithmetic  10.4 us (3%)
  between operations  7.01 us (2%)
    pallas_call x1, Pallas kernels, collect(): pl.pallas_call(functools.partial(collect_body, cap, ch), out_shape=[jax.S...  173 us
    pallas_call x1, Pallas kernels, spread(): pl.pallas_call(functools.partial(spread_body, cap, n_third), out_shape=[j...  104 us
    pallas_call x1, Pallas kernels, block_step(): pl.pallas_call(functools.partial(block_body, loss_factor), out_shape=[jax...  68 us
    pallas_call x1, Pallas kernels, adam(): pl.pallas_call(functools.partial(adam_body, group), grid_spec=pltpu.Prefe...  35.5 us

profile of v2, /device:TPU:0, one launch (start us, length us, event | category | flops | bytes accessed | tf_op | source)
XLA Modules:
  0.0 401.5 jit_solution(5248925495315005968)
XLA Ops:
  0.6 1.3 compare_convert_fusion
  1.9 1.3 compare_select_fusion.1.row_ref
  3.2 0.7 broadcast_remainder_fusion.1
  3.9 0.1 mul.85
  4.0 0.1 copy.23
  4.1 0.1 rem.136
  4.2 0.8 convert_reduce_fusion
  4.9 0.7 dynamic-slice_reduce_fusion.where_ref
  6.3 0.1 fusion.64
  7.0 0.1 pad.3.clone
  7.1 0.1 pad.4.clone
  7.2 0.1 maximum_maximum_fusion
  7.2 0.7 compare_convert_fusion.1
  7.9 0.1 reshape.274
  8.0 0.1 reduce_sum.89
  8.1 0.6 reduce_max.9
  10.1 0.0 copy-start.1
  10.1 105.3 %conditional.2 = ((bf16[8,36,256,256]{3,2,1,0:T(8,128)(2,1)}, bf16[8,64,128]{2,1,0:T(8,128)(2,1)S(1)}, f32[64,128]{1,0:T(8,128)S(1)}, bf16[32,256]{1,0:T(8,128)(...) conditional(s32[]{:T(128)} %clamp.4, (s32[36]{0:T(128)}, ...), branch_computations={%region_5.7_spmd, %region_7.9_spmd, %region_9.11_spmd} | conditional | flops 3852 | bytes 10664 | solution.py:1733
  10.1 1.2 select_reduce_fusion.slot_ref
  11.3 103.9 %spread.3 = (bf16[8,36,256,256]{3,2,1,0:T(8,128)(2,1)}, bf16[8,64,128]{2,1,0:T(8,128)(2,1)S(1)}, f32[64,128]{1,0:T(8,128)S(1)}, bf16[32,256]{1,0:T(8,128)(2,1)S(...) custom-call(s32[36]{0:T(128)} %select_reduce_fusion.slot_ref, ...), custom_call_target="tpu_custom_call" | custom-call | tf_op jit(solution)/shard_map/cond/branch_0_fun/spread/pallas_call | solution.py:889
  115.4 0.1 copy.24
  115.5 0.1 broadcast_add_fusion
  115.6 0.1 add.444
  115.7 0.0 copy-done.1
  115.7 0.2 select_reduce_fusion.3
  115.9 0.6 slice.47.place_ref
  116.5 0.1 multiply_sine_fusion
  116.7 0.6 pad_maximum_fusion.spot_ref
  117.3 0.0 copy-start
  117.3 68.0 %block_step.1 = (bf16[64,256,256]{2,1,0:T(8,128)(2,1)}, f32[64,128]{1,0:T(8,128)S(1)}, f32[8,48,128]{2,1,0:T(8,128)S(1)}, f32[8,128]{1,0:T(8,128)S(1)}) custom-call(s32[192]{0:T(256)} %slice.47.place_ref, bf16[288,256,256]{2,1,0:T(8,128)(2,1)} %bitcast.12, bf16[16,256]{1,0:T(8,128)(2,1)} %bitcast.14, f32[16,256]{1,0:T(8,128)} %bitcast.13, ...), custom_call_target="tpu_custom_call" | custom-call | flops 19327352832 | bytes 50331648 | tf_op jit(solution)/shard_map/block_step/pallas_call | solution.py:424
  185.4 0.0 copy-done
  185.4 175.2 %conditional.3 = (f32[8,128]{1,0:T(8,128)S(1)}, bf16[36,256,256]{2,1,0:T(8,128)(2,1)}, bf16[24,32,256]{2,1,0:T(8,128)(2,1)S(1)}, f32[4379,128]{1,0:T(8,128)}, f32[8,128]{1,0:T(8,128)S(1)}) conditional(s32[]{:T(128)} %clamp.4, (s32[288]{0:T(512)S(1)}, s32[288]{0:T(512)S(1)}, pred[288]{0:T(512)(128)(4,1)S(1)}, ...), branch_computations={%region_11.13_spmd.clone, %region_13.15_spmd.clone, %region_15.17_... | conditional | flops 17603 | bytes 33312 | solution.py:1751
  185.5 0.6 fusion.left_ref
  186.1 0.6 fusion.10.right_ref
  186.6 0.6 reduce_sum.93
  187.3 173.4 %collect.12 = (bf16[36,256,256]{2,1,0:T(8,128)(2,1)}, bf16[24,32,256]{2,1,0:T(8,128)(2,1)S(1)}, f32[4379,128]{1,0:T(8,128)}, f32[8,128]{1,0:T(8,128)S(1)}, f32[8,128]{1,0:T(8,128)S(1)}) custom-call(s32[288]{0:T(512)} %fusion.left_ref, s32[288]{0:T(512)} %fusion.10.right_ref, s32[36]{0:T(128)} %get-tuple-element.1895.row_ref, s32[36]{0:T(128)} %get-tuple-element.1896.col_ref, ...), custom_call_target="tpu_custom_call" | custom-call | tf_op jit(solution)/shard_map/cond/branch_0_fun/collect/pallas_call | solution.py:1458
  360.7 35.5 %adam.1 = (f32[36,256,256]{2,1,0:T(8,128)}, f32[36,256,256]{2,1,0:T(8,128)}, f32[36,256,256]{2,1,0:T(8,128)}, f32[4379,128]{1,0:T(8,128)}, f32[4379,128]{1,0:T(8,128)}, /*index=5*/f32[4379,128]{1,0:T(8,128)}) custom-call(s32[36]{0:T(128)} %dynamic-slice_reduce_fusion.where_ref, s32[36]{0:T(128)} %compare_select_fusion.1.row_ref, ...), custom_call_target="tpu_custom_call" | custom-call | tf_op jit(solution)/shard_map/adam/pallas_call | solution.py:589
  396.2 0.5 slice.48
  397.4 0.5 slice.49
  398.6 0.6 sqrt_reduce_fusion
  (17 shorter events, 0.1 us)
Async XLA Ops:
  10.1 105.6 %copy-start.1 = (s32[288]{0:T(512)S(1)}, s32[288]{0:T(512)}, u32[]{:S(2)}) copy-start(s32[288]{0:T(512)} %param.22) | copy-start | bytes 3460
  117.3 68.1 %copy-start = (f32[4379,128]{1,0:T(8,128)S(1)}, f32[4379,128]{1,0:T(8,128)}, u32[]{:S(2)}) copy-start(f32[4379,128]{1,0:T(8,128)} %row_master_ref.1) | copy-start | bytes 6726148
